TPU v7x, 512 devices: a whole 4x8x8 slice. The times are simulated.
512 devices in a mesh: gx: 8 (over y), gy: 4 (over x), gz: 16 (over z, core).
Axes of the slice: x: 4, y: 8, z: 8, core: 2. Of those that a mesh axis runs over, the one named last changes fastest.
Arguments:
- patches: float32 [1024, 6, 16, 256], P(('gx', 'gy', 'gz')), may hold values from -2 to 6, as said below
- new_owner: int32 [1024], P(('gx', 'gy')), may hold values from 0 to 511, as said below
- new_slot: int32 [1024], P(('gx', 'gy')), may hold values from 0 to 3, as said below
Outputs:
- new_state: float32 [2048, 6, 16, 256], P(('gx', 'gy', 'gz'))
Inputs may be any that keep to these rules, and one draw needn't show every extreme that they name: `patches`: each cell has density and pressure in [0.5, 2], velocity components in [-1, 1] and mass fraction in [0, 1]; momenta, energy and species density follow from these with the energy law of the steps. `new_owner`: A patch's new owner is its old owner p // 2 or the device whose index along gz differs from the old owner's in its lowest bit; within each group along gz the patches, in order of id, go to the group's devices in order of device index in contiguous runs; a device receives 0 to 4 patches, and in every group some device receives exactly 4. `new_slot`: the position of the patch in its new owner's run, so each device's used slots are 0 up to its count minus one.
All inputs are finite; a program needn't handle non-finite values.
Results may differ from a plain program's by a relative error of at most 0.0001.
Values sent between devices are 32-bit elements; how exact they have to be, the bound alone decides.
No kernel may reach another device: no remote copies, remote signals or barrier semaphores. Data moves between devices by JAX's collectives and lax.ppermute only.
A program may use at most 64 MiB of HBM per device.

v0:
```python
import jax
import jax.numpy as jnp
from jax import lax
from jax.sharding import PartitionSpec as P

EDGE = 16
GHOST = 4
CAP = 4


GAMMA = 5.0 / 3.0
STEP_RATIO = 0.08


def with_halo(value, sides, width):
    for axis, dim in sides:
        count, length = (lax.axis_size(axis), value.shape[dim])
        up = [(i, (i + 1) % count) for i in range(count)]
        down = [(j, i) for i, j in up]
        last = lax.slice_in_dim(value, length - width, length, axis=dim)
        leading = lax.slice_in_dim(value, 0, width, axis=dim)
        before = lax.ppermute(last, axis, up)
        after = lax.ppermute(leading, axis, down)
        value = jnp.concatenate([before, value, after], axis=dim)
    return value


def median_three(first, second, third):
    return jnp.maximum(jnp.minimum(first, second), jnp.minimum(jnp.maximum(first, second), third))


def to_primitive(conserved):
    density = conserved[0]
    velocity = conserved[1:4] / density
    pressure = (GAMMA - 1.0) * (conserved[4] - 0.5 * density * jnp.sum(velocity * velocity, axis=0))
    fraction = conserved[5] / density
    return jnp.concatenate([density[None], velocity, pressure[None], fraction[None]], axis=0)


def face_flux(primitive, normal):
    density = primitive[0]
    velocity = primitive[1:4]
    pressure = primitive[4]
    fraction = primitive[5]
    speed = velocity[normal]
    energy = pressure / (GAMMA - 1.0) + 0.5 * density * jnp.sum(velocity * velocity, axis=0)
    conserved = jnp.concatenate(
        [density[None], density * velocity, energy[None], (density * fraction)[None]], axis=0
    )
    flux = conserved * speed
    flux = flux.at[1 + normal].add(pressure)
    flux = flux.at[4].add(pressure * speed)
    signal = jnp.abs(speed) + jnp.sqrt(GAMMA * pressure / density)
    return (conserved, flux, signal)


def sweep(extended, normal):
    primitive = to_primitive(extended)
    length = primitive.shape[1]
    interior_count = length - 8
    left_cell = primitive[:, 2 : length - 3]
    right_cell = primitive[:, 3 : length - 2]
    face = (
        37.0 * (left_cell + right_cell)
        - 8.0 * (primitive[:, 1 : length - 4] + primitive[:, 4 : length - 1])
        + (primitive[:, 0 : length - 5] + primitive[:, 5:length])
    ) / 60.0
    face = jnp.clip(face, jnp.minimum(left_cell, right_cell), jnp.maximum(left_cell, right_cell))
    centre = primitive[:, 3 : length - 3]
    left_jump = centre - face[:, :-1]
    right_jump = face[:, 1:] - centre
    zeros = jnp.zeros_like(centre)
    right_limited = median_three(zeros, right_jump, 2.0 * left_jump)
    left_limited = median_three(zeros, left_jump, 2.0 * right_jump)
    plus_state = centre + right_limited
    minus_state = centre - left_limited
    left_state = plus_state[:, 0 : interior_count + 1]
    right_state = minus_state[:, 1 : interior_count + 2]
    left_cons, left_flux, left_signal = face_flux(left_state, normal)
    right_cons, right_flux, right_signal = face_flux(right_state, normal)
    signal = jnp.maximum(left_signal, right_signal)
    flux = 0.5 * (left_flux + right_flux) - 0.5 * signal * (right_cons - left_cons)
    return flux[:, 1:] - flux[:, :-1]


def advance_patch(package):
    fields_count = package.shape[0]
    plane = package.shape[2]
    side_cells = EDGE
    depth = GHOST
    interior = package[:, :side_cells]
    pieces = [package[:, side_cells + k * depth : side_cells + (k + 1) * depth] for k in range(6)]
    cube = interior.reshape(fields_count, side_cells, side_cells, side_cells)
    div_x = sweep(jnp.concatenate([pieces[0], interior, pieces[1]], axis=1), 0)
    y_major = cube.transpose(0, 2, 1, 3).reshape(fields_count, side_cells, plane)
    div_y = sweep(jnp.concatenate([pieces[2], y_major, pieces[3]], axis=1), 1)
    div_y = (
        div_y.reshape(fields_count, side_cells, side_cells, side_cells)
        .transpose(0, 2, 1, 3)
        .reshape(fields_count, side_cells, plane)
    )
    z_major = cube.transpose(0, 3, 1, 2).reshape(fields_count, side_cells, plane)
    div_z = sweep(jnp.concatenate([pieces[4], z_major, pieces[5]], axis=1), 2)
    div_z = (
        div_z.reshape(fields_count, side_cells, side_cells, side_cells)
        .transpose(0, 2, 3, 1)
        .reshape(fields_count, side_cells, plane)
    )
    return interior - STEP_RATIO * (div_x + div_y + div_z)


def relocate(payload, new_owner, new_slot):
    members = lax.axis_size("gz")
    slots = payload.shape[0]
    spread = lax.all_to_all(payload, "gz", split_axis=3, concat_axis=0, tiled=True)
    target = new_owner % members * CAP + new_slot
    wanted = lax.broadcasted_iota(jnp.int32, (members * CAP, members * slots), 0)
    match = target[None, :] == wanted
    source = jnp.sum(jnp.where(match, lax.broadcasted_iota(jnp.int32, match.shape, 1), 0), axis=1)
    filled = jnp.any(match, axis=1)
    picked = jnp.take(spread, source, axis=0)
    picked = jnp.where(filled[:, None, None, None], picked, jnp.zeros_like(picked))
    gathered = lax.all_to_all(picked, "gz", split_axis=0, concat_axis=3, tiled=True)
    mine = lax.dynamic_slice_in_dim(filled.reshape(members, CAP), lax.axis_index("gz"), 1, 0)[0]
    return (gathered, mine)


def on_device(patches, new_owner, new_slot):
    slots = patches.shape[0]
    fields_count = patches.shape[1]
    side_cells = patches.shape[2]
    plane = patches.shape[3]
    block = patches.transpose(1, 0, 2, 3).reshape(fields_count, slots * side_cells, plane)
    cube = block.reshape(fields_count, slots * side_cells, side_cells, side_cells)
    y_major = cube.transpose(0, 2, 1, 3).reshape(fields_count, side_cells, slots * plane)
    z_major = cube.transpose(0, 3, 1, 2).reshape(fields_count, side_cells, slots * plane)
    ext_x = with_halo(block, (("gx", 1),), GHOST)
    ext_y = with_halo(y_major, (("gy", 1),), GHOST)
    ext_z = with_halo(z_major, (("gz", 1),), GHOST)
    lower_y = ext_y[:, :GHOST].reshape(fields_count, GHOST, slots, plane)
    upper_y = ext_y[:, side_cells + GHOST :].reshape(fields_count, GHOST, slots, plane)
    lower_z = ext_z[:, :GHOST].reshape(fields_count, GHOST, slots, plane)
    upper_z = ext_z[:, side_cells + GHOST :].reshape(fields_count, GHOST, slots, plane)
    packages = []
    for slot_index in range(slots):
        start = slot_index * side_cells
        packages.append(
            jnp.concatenate(
                [
                    block[:, start : start + side_cells],
                    ext_x[:, start : start + GHOST],
                    ext_x[:, start + side_cells + GHOST : start + side_cells + 2 * GHOST],
                    lower_y[:, :, slot_index],
                    upper_y[:, :, slot_index],
                    lower_z[:, :, slot_index],
                    upper_z[:, :, slot_index],
                ],
                axis=1,
            )
        )
    packages = jnp.stack(packages, axis=0)
    moved, mine = relocate(packages, new_owner, new_slot)
    neutral = jnp.array([1.0, 0.0, 0.0, 0.0, 1.0, 0.0], jnp.float32)[None, :, None, None]
    ready = jnp.where(mine[:, None, None, None], moved, jnp.broadcast_to(neutral, moved.shape))
    advanced = lax.map(advance_patch, ready)
    return jnp.where(mine[:, None, None, None], advanced, jnp.zeros_like(advanced))


def solution(mesh):
    in_specs = (P(("gx", "gy", "gz"), None, None, None), P(("gx", "gy")), P(("gx", "gy")))
    out_specs = P(("gx", "gy", "gz"), None, None, None)
    return jax.shard_map(
        on_device, mesh=mesh, in_specs=in_specs, out_specs=out_specs, check_vma=False
    )
```

profile of v0, /device:TPU:1, one launch (start us, length us, event | category | flops | bytes accessed | tf_op | source)
XLA Modules:
  0.0 139.0 jit_solution(298762258660932456)
XLA Ops:
  1.4 1.7 %fusion.57 = (f32[6,4,512]{1,2,0:T(8,128)}, f32[6,4,512]{1,2,0:T(8,128)S(1)}) fusion(f32[6,16,512]{1,2,0:T(8,128)S(1)} %bitcast.201), kind=kLoop, calls=%fused_computation.188 | loop fusion | bytes 196608 | tf_op jit(solution)/shard_map/slice | solution.py:21
  3.1 1.9 %copy.98 = f32[6,4,512]{2,1,0:T(4,128)S(1)} copy(f32[6,4,512]{1,2,0:T(8,128)} %get-tuple-element.299) | data formatting | bytes 98304
  5.0 6.9 %collective-permute-start.4 = (f32[6,4,512]{2,1,0:T(4,128)S(1)}, f32[6,4,512]{2,1,0:T(4,128)S(1)}, u32[]{:S(2)}, u32[]{:S(2)}) collective-permute-start(f32[6,4,512]{2,1,0:T(4,128)S(1)} %copy.98), channel_id=1, source_target_pairs={{1,0},{2,1},{3,2},{4,3},{5,4},{6,5},{7,6},{8,7},{9,8},{10,9},{11,1... | collective-permute-start | bytes 147464 | tf_op jit(solution)/shard_map/ppermute | solution.py:23
  12.9 1.1 reshape.479
  13.9 1.9 %collective-permute-start.2 = (f32[6,4,512]{2,1,0:T(4,128)S(1)}, f32[6,4,512]{2,1,0:T(4,128)S(1)}, u32[]{:S(2)}, u32[]{:S(2)}) collective-permute-start(f32[6,4,512]{2,1,0:T(4,128)S(1)} %get-tuple-element.307), channel_id=1, source_target_pairs={{16,0},{32,16},{48,32},{0,48},{17,1},{33,17},{49,33},{1,49},{18,2}... | collective-permute-start | bytes 147464 | tf_op jit(solution)/shard_map/ppermute | solution.py:23
  15.9 3.4 %collective-permute-start.1 = (f32[6,4,512]{2,1,0:T(4,128)S(1)}, f32[6,4,512]{2,1,0:T(4,128)S(1)}, u32[]{:S(2)}, u32[]{:S(2)}) collective-permute-start(f32[6,4,512]{2,1,0:T(4,128)S(1)} %get-tuple-element.308), channel_id=1, source_target_pairs={{0,16},{16,32},{32,48},{48,0},{1,17},{17,33},{33,49},{49,1},{2,18}... | collective-permute-start | bytes 147464 | tf_op jit(solution)/shard_map/ppermute | solution.py:22
  19.3 1.9 %collective-permute-start = (f32[6,4,256]{2,1,0:T(4,128)S(1)}, f32[6,4,256]{2,1,0:T(4,128)S(1)}, u32[]{:S(2)}, u32[]{:S(2)}) collective-permute-start(f32[6,4,256]{2,1,0:T(4,128)S(1)} %get-tuple-element.304), channel_id=1, source_target_pairs={{0,64},{64,128},{128,192},{192,256},{256,320},{320,384},{384,448},... | collective-permute-start | bytes 73736 | tf_op jit(solution)/shard_map/ppermute | solution.py:22
  21.2 4.6 %collective-permute-start.5 = (f32[6,4,256]{2,1,0:T(4,128)S(1)}, f32[6,4,256]{2,1,0:T(4,128)S(1)}, u32[]{:S(2)}, u32[]{:S(2)}) collective-permute-start(f32[6,4,256]{2,1,0:T(4,128)S(1)} %get-tuple-element.302), channel_id=1, source_target_pairs={{64,0},{128,64},{192,128},{256,192},{320,256},{384,320},{448,384},... | collective-permute-start | bytes 73736 | tf_op jit(solution)/shard_map/ppermute | solution.py:23
  26.9 1.0 copy.87
  28.0 3.8 %reshape.493 = f32[16,1,7680]{2,1,0:T(1,128)} reshape(f32[256,6,2,40]{3,2,1,0:T(2,128)S(1)} %bitcast.209) | data formatting | bytes 983040
  31.8 9.5 %all-to-all-start = ((f32[16,1,7680]{2,1,0:T(1,128)}), f32[16,1,7680]{2,1,0:T(1,128)S(1)}, u32[]{:S(2)}, u32[]{:S(2)}) async-start(f32[16,1,7680]{2,1,0:T(1,128)} %reshape.493), calls=%async_computation | async-start | bytes 983040 | tf_op jit(solution)/shard_map/all_to_all | solution.py:115
  41.6 16.4 %all-to-all-done = f32[16,1,7680]{2,1,0:T(1,128)S(1)} async-done(((f32[16,1,7680]{2,1,0:T(1,128)}), f32[16,1,7680]{2,1,0:T(1,128)S(1)}, u32[]{:S(2)}, u32[]{:S(2)}) %all-to-all-start) | async-done | bytes 491552 | tf_op jit(solution)/shard_map/all_to_all | solution.py:115
  58.4 1.7 %reduce.36 = f32[16,7680]{1,0:T(8,128)S(1)} reduce(f32[16,1,7680]{2,1,0:T(1,128)S(1)} %all-to-all-done, f32[]{:T(128)} %broadcast.397), dimensions={1}, to_apply=%all_to_all.26.reduce_sub_computation | reduce | bytes 983044 | tf_op jit(solution)/shard_map/all_to_all | solution.py:115
  60.1 2.7 %reshape.494 = f32[256,6,2,40]{3,2,1,0:T(2,128)S(1)} reshape(f32[16,7680]{1,0:T(8,128)S(1)} %reduce.36) | data formatting | bytes 983040
  63.2 2.4 %gather_fusion = f32[64,6,40,16]{2,3,1,0:T(8,128)} fusion(f32[32,6,40,16]{2,3,1,0:T(8,128)S(1)} %bitcast.200, s32[1024]{0:T(1024)S(1)} %pad_clamp_fusion), kind=kCustom, calls=%fused_computation | custom fusion | bytes 1966336 | tf_op jit(solution)/shard_map/jit(_take)/gather | solution.py:121
  65.6 2.3 %fusion.65 = f32[64,6,16,40]{3,2,1,0:T(8,128)S(1)} fusion(f32[64,6,40,16]{2,3,1,0:T(8,128)} %gather_fusion, pred[64]{0:T(512)(128)(4,1)S(1)} %compare_and_fusion, pred[64]{0:T(512)(128)(4,1)S(1)} %fusion.51), kind=kLoop, calls=%fused_computation.196 | loop fusion | flops 491520 | bytes 1966208
  67.9 3.9 %reshape.495 = f32[16,1,15360]{2,1,0:T(1,128)} reshape(f32[64,6,16,40]{3,2,1,0:T(8,128)S(1)} %fusion.65) | data formatting | bytes 1966080
  71.9 3.8 %all-to-all-start.1 = ((f32[16,1,15360]{2,1,0:T(1,128)}), f32[16,1,15360]{2,1,0:T(1,128)S(1)}, u32[]{:S(2)}, u32[]{:S(2)}) async-start(f32[16,1,15360]{2,1,0:T(1,128)} %reshape.495), calls=%async_computation.1 | async-start | bytes 1966080 | tf_op jit(solution)/shard_map/all_to_all | solution.py:123
  75.8 25.7 %all-to-all-done.1 = f32[16,1,15360]{2,1,0:T(1,128)S(1)} async-done(((f32[16,1,15360]{2,1,0:T(1,128)}), f32[16,1,15360]{2,1,0:T(1,128)S(1)}, u32[]{:S(2)}, u32[]{:S(2)}) %all-to-all-start.1) | async-done | bytes 983072 | tf_op jit(solution)/shard_map/all_to_all | solution.py:123
  101.4 4.1 %reduce.37 = f32[16,15360]{1,0:T(8,128)} reduce(f32[16,1,15360]{2,1,0:T(1,128)S(1)} %all-to-all-done.1, f32[]{:T(128)} %broadcast.397), dimensions={1}, to_apply=%all_to_all.30.reduce_sub_computation | reduce | bytes 1966084 | tf_op jit(solution)/shard_map/all_to_all | solution.py:123
  105.6 3.8 %reshape.496 = f32[64,6,16,40]{3,2,1,0:T(8,128)S(1)} reshape(f32[16,15360]{1,0:T(8,128)} %reduce.37) | data formatting | bytes 1966080
  110.4 1.9 %copy.91 = f32[4,6,40,256]{3,2,1,0:T(8,128)} copy(f32[4,6,40,256]{2,3,1,0:T(8,128)S(1)} %bitcast_select_fusion) | data formatting | bytes 1966080 | tf_op jit(solution)/shard_map/while | solution.py:165
  112.4 24.8 %while.26 = (s32[]{:T(128)}, f32[4,6,16,256]{3,2,1,0:T(8,128)}, f32[4,6,40,256]{3,2,1,0:T(8,128)}) while((s32[]{:T(128)}, f32[4,6,16,256]{3,2,1,0:T(8,128)}, f32[4,6,40,256]{3,2,1,0:T(8,128)}) %tuple.195), condition=%wide.region_12.13_spmd.clone, body=%wide.region_2.12_spmd.sunk.clone | while | flops 5323778 | bytes 17858096 | solution.py:165
  137.2 1.9 %broadcast_select_fusion = f32[4,6,16,256]{3,2,1,0:T(8,128)} fusion(f32[4,6,16,256]{3,2,1,0:T(8,128)} %get-tuple-element.216, pred[4]{0:T(512)(128)(4,1)S(1)} %dynamic-slice_bitcast_fusion.1), kind=kLoop, calls=%fused_computation.162 | loop fusion | flops 98304 | bytes 786436 | tf_op jit(solution)/shard_map/jit(_where)/select_n | solution.py:166
  (329 shorter events, 28.7 us)
Async XLA Ops:
  5.0 16.2 %collective-permute-start.4 = (f32[6,4,512]{2,1,0:T(4,128)S(1)}, f32[6,4,512]{2,1,0:T(4,128)S(1)}, u32[]{:S(2)}, u32[]{:S(2)}) collective-permute-start(f32[6,4,512]{2,1,0:T(4,128)S(1)} %copy.98), channel_id=1, source_target_pairs={{1,0},{2,1},{3,2},{4,3},{5,4},{6,5},{7,6},{8,7},{9,8},{10,9},{11,1... | collective-permute-start | bytes 147464 | tf_op jit(solution)/shard_map/ppermute | solution.py:23
  12.4 13.6 %collective-permute-start.3 = (f32[6,4,512]{2,1,0:T(4,128)S(1)}, f32[6,4,512]{2,1,0:T(4,128)S(1)}, u32[]{:S(2)}, u32[]{:S(2)}) collective-permute-start(f32[6,4,512]{2,1,0:T(4,128)S(1)} %copy.96), channel_id=1, source_target_pairs={{0,1},{1,2},{2,3},{3,4},{4,5},{5,6},{6,7},{7,8},{8,9},{9,10},{10,1... | collective-permute-start | bytes 147464 | tf_op jit(solution)/shard_map/ppermute | solution.py:22
  13.9 12.1 %collective-permute-start.2 = (f32[6,4,512]{2,1,0:T(4,128)S(1)}, f32[6,4,512]{2,1,0:T(4,128)S(1)}, u32[]{:S(2)}, u32[]{:S(2)}) collective-permute-start(f32[6,4,512]{2,1,0:T(4,128)S(1)} %get-tuple-element.307), channel_id=1, source_target_pairs={{16,0},{32,16},{48,32},{0,48},{17,1},{33,17},{49,33},{1,49},{18,2}... | collective-permute-start | bytes 147464 | tf_op jit(solution)/shard_map/ppermute | solution.py:23
  15.9 10.3 %collective-permute-start.1 = (f32[6,4,512]{2,1,0:T(4,128)S(1)}, f32[6,4,512]{2,1,0:T(4,128)S(1)}, u32[]{:S(2)}, u32[]{:S(2)}) collective-permute-start(f32[6,4,512]{2,1,0:T(4,128)S(1)} %get-tuple-element.308), channel_id=1, source_target_pairs={{0,16},{16,32},{32,48},{48,0},{1,17},{17,33},{33,49},{49,1},{2,18}... | collective-permute-start | bytes 147464 | tf_op jit(solution)/shard_map/ppermute | solution.py:22
  19.3 7.1 %collective-permute-start = (f32[6,4,256]{2,1,0:T(4,128)S(1)}, f32[6,4,256]{2,1,0:T(4,128)S(1)}, u32[]{:S(2)}, u32[]{:S(2)}) collective-permute-start(f32[6,4,256]{2,1,0:T(4,128)S(1)} %get-tuple-element.304), channel_id=1, source_target_pairs={{0,64},{64,128},{128,192},{192,256},{256,320},{320,384},{384,448},... | collective-permute-start | bytes 73736 | tf_op jit(solution)/shard_map/ppermute | solution.py:22
  21.2 5.5 %collective-permute-start.5 = (f32[6,4,256]{2,1,0:T(4,128)S(1)}, f32[6,4,256]{2,1,0:T(4,128)S(1)}, u32[]{:S(2)}, u32[]{:S(2)}) collective-permute-start(f32[6,4,256]{2,1,0:T(4,128)S(1)} %get-tuple-element.302), channel_id=1, source_target_pairs={{64,0},{128,64},{192,128},{256,192},{320,256},{384,320},{448,384},... | collective-permute-start | bytes 73736 | tf_op jit(solution)/shard_map/ppermute | solution.py:23
  26.8 14.5 %copy-start.1 = (s32[32]{0:T(128)S(1)}, s32[32]{0:T(128)}, u32[]{:S(2)}) copy-start(s32[32]{0:T(128)} %param.32) | copy-start | bytes 388
  26.9 14.5 %copy-start.2 = (s32[32]{0:T(128)S(1)}, s32[32]{0:T(128)}, u32[]{:S(2)}) copy-start(s32[32]{0:T(128)} %param.31) | copy-start | bytes 388
  31.8 26.1 %all-to-all-start = ((f32[16,1,7680]{2,1,0:T(1,128)}), f32[16,1,7680]{2,1,0:T(1,128)S(1)}, u32[]{:S(2)}, u32[]{:S(2)}) async-start(f32[16,1,7680]{2,1,0:T(1,128)} %reshape.493), calls=%async_computation | async-start | bytes 983040 | tf_op jit(solution)/shard_map/all_to_all | solution.py:115
  71.9 29.6 %all-to-all-start.1 = ((f32[16,1,15360]{2,1,0:T(1,128)}), f32[16,1,15360]{2,1,0:T(1,128)S(1)}, u32[]{:S(2)}, u32[]{:S(2)}) async-start(f32[16,1,15360]{2,1,0:T(1,128)} %reshape.495), calls=%async_computation.1 | async-start | bytes 1966080 | tf_op jit(solution)/shard_map/all_to_all | solution.py:123
  109.3 0.7 copy-start
where the time goes:
time: 142 us; the launch traced here: 139 us
  local copies, waits for them, and re-layouts  42.8 us (30%)
  waiting for transfers between devices  42.3 us (30%)
  starting transfers between devices  32 us (23%)
  other arithmetic  19.8 us (14%)
  loops' own time  1.71 us (1%)
    all_to_all x1, waiting for transfers between devices, relocate(): lax.all_to_all(picked, 'gz', split_axis=0, concat_axis=3, tiled=True)  25.7 us
    unnamed x13, local copies, waits for them, and re-layouts  17.9 us
    all_to_all x1, waiting for transfers between devices, relocate(): lax.all_to_all(payload, 'gz', split_axis=3, concat_axis=0, tiled=True)  16.4 us
    ppermute x3, starting transfers between devices, with_halo(): after = lax.ppermute(leading, axis, down)  13.4 us
    all_to_all x1, starting transfers between devices, relocate(): lax.all_to_all(payload, 'gz', split_axis=3, concat_axis=0, tiled=True)  9.55 us
    ppermute x3, starting transfers between devices, with_halo(): before = lax.ppermute(last, axis, up)  5.29 us
    all_to_all x1, other arithmetic, relocate(): lax.all_to_all(picked, 'gz', split_axis=0, concat_axis=3, tiled=True)  4.12 us
    squeeze x4, local copies, waits for them, and re-layouts, on_device(): advanced = lax.map(advance_patch, ready)  3.84 us
  transfers between devices with their start and end apart: 8, of which 3 were waited for; matrix products, arithmetic and copies ran while one was open for 2% of the time, Pallas kernels for 0%

commit v1 on v0

v1 whole, which is shorter than its diff:
```python
import functools

import jax
import jax.numpy as jnp
from jax import lax
from jax.experimental import pallas as pl
from jax.experimental.pallas import tpu as pltpu
from jax.sharding import PartitionSpec as P

EDGE = 16
GHOST = 4
CAP = 4
FIELDS = 6
PLANE = EDGE * EDGE
STRIP = GHOST * EDGE

STEP_RATIO = 0.08
VMEM = pl.BlockSpec(memory_space=pltpu.VMEM)
SMEM = pl.BlockSpec(memory_space=pltpu.SMEM)


def to_primitive(u):
    density, mom_x, mom_y, mom_z, energy, species = u
    inverse = 1.0 / density
    vel_x, vel_y, vel_z = mom_x * inverse, mom_y * inverse, mom_z * inverse
    kinetic = 0.5 * (mom_x * vel_x + mom_y * vel_y + mom_z * vel_z)
    pressure = (2.0 / 3.0) * (energy - kinetic)
    return [density, vel_x, vel_y, vel_z, pressure, species * inverse]


def median_zero(second, third):
    return jnp.maximum(jnp.minimum(second, 0.0), jnp.minimum(jnp.maximum(second, 0.0), third))


def side_terms(state, normal):
    density, pressure = state[0], state[4]
    ratio = pressure / density
    speed = state[1 + normal]
    square = state[1] * state[1] + state[2] * state[2] + state[3] * state[3]
    specific = 1.5 * ratio + 0.5 * square
    signal = jnp.abs(speed) + jnp.sqrt((5.0 / 3.0) * ratio)
    return speed, specific, signal


def sweep(primitive, normal, at):
    plus, minus = [], []
    for value in primitive:
        after = at(value, 1)
        face = 37.0 * (value + after) - 8.0 * (at(value, -1) + at(value, 2)) + (at(value, -2) + at(value, 3))
        face = face * (1.0 / 60.0)
        face = jnp.minimum(jnp.maximum(face, jnp.minimum(value, after)), jnp.maximum(value, after))
        left_jump = value - at(face, -1)
        right_jump = face - value
        plus.append(value + median_zero(right_jump, 2.0 * left_jump))
        minus.append(at(value - median_zero(left_jump, 2.0 * right_jump), 1))
    left_speed, left_specific, left_signal = side_terms(plus, normal)
    right_speed, right_specific, right_signal = side_terms(minus, normal)
    signal = jnp.maximum(left_signal, right_signal)
    left_weight = 0.5 * plus[0] * (left_speed + signal)
    right_weight = 0.5 * minus[0] * (right_speed - signal)
    flux = [left_weight + right_weight]
    for k in (1, 2, 3):
        flux.append(left_weight * plus[k] + right_weight * minus[k])
    flux[1 + normal] = flux[1 + normal] + 0.5 * (plus[4] + minus[4])
    flux.append(
        left_weight * left_specific
        + right_weight * right_specific
        + 0.5 * (plus[4] * left_speed + minus[4] * right_speed)
    )
    flux.append(left_weight * plus[5] + right_weight * minus[5])
    return [f - at(f, -1) for f in flux]


def exchange_lanes(rows):
    source = lax.broadcasted_iota(jnp.int32, (PLANE, PLANE), 0)
    target = lax.broadcasted_iota(jnp.int32, (PLANE, PLANE), 1)
    wanted = (target % EDGE) * EDGE + target // EDGE
    swap = jnp.where(source == wanted, 1.0, 0.0).astype(jnp.bfloat16)
    total = None
    for _ in range(3):
        part = rows.astype(jnp.bfloat16)
        moved = jnp.dot(part, swap, preferred_element_type=jnp.float32)
        total = moved if total is None else total + moved
        rows = rows - part.astype(jnp.float32)
    return total


def pack_kernel(u_ref, prim_ref, prim_z_ref, x_up, x_down, y_up, y_down, z_up, z_down):
    slots = u_ref.shape[0]
    for p in range(slots):
        for q, value in enumerate(to_primitive([u_ref[p, q] for q in range(FIELDS)])):
            prim_ref[p, q] = value
    flat = prim_ref[...].reshape(slots * FIELDS * EDGE, PLANE)
    prim_z_ref[...] = exchange_lanes(flat).reshape(slots, FIELDS, EDGE, PLANE)
    x_up[...] = prim_ref[slots - 1, :, EDGE - GHOST :, :]
    x_down[...] = prim_ref[0, :, :GHOST, :]
    for p in range(slots):
        lanes = slice(p * STRIP, (p + 1) * STRIP)
        y_up[:, :, lanes] = prim_ref[p, :, :, PLANE - STRIP :]
        y_down[:, :, lanes] = prim_ref[p, :, :, :STRIP]
        z_up[:, :, lanes] = prim_z_ref[p, :, :, PLANE - STRIP :]
        z_down[:, :, lanes] = prim_z_ref[p, :, :, :STRIP]


def lane_at(value, k):
    width = value.shape[1]
    return pltpu.roll(value, (-k * EDGE) % width, 1)


def row_at(value, k):
    height = value.shape[0]
    return pltpu.roll(value, (-k) % height, 0)


def update_kernel(u_ref, prim_ref, prim_z_ref, x_low, x_high, y_low, y_high, z_low, z_high, out_ref, change_ref):
    slots = u_ref.shape[0]
    for p in range(slots):
        lanes = slice(p * STRIP, (p + 1) * STRIP)
        for half in range(2):
            rows = slice(half * 8, half * 8 + 8)
            lines = [
                jnp.concatenate([z_low[q, rows, lanes], prim_z_ref[p, q, rows, :], z_high[q, rows, lanes]], axis=1)
                for q in range(FIELDS)
            ]
            for q, value in enumerate(sweep(lines, 2, lane_at)):
                change_ref[p, q, rows, :] = value[:, STRIP : STRIP + PLANE]
    flat = change_ref[...].reshape(slots * FIELDS * EDGE, PLANE)
    change_ref[...] = exchange_lanes(flat).reshape(slots, FIELDS, EDGE, PLANE)
    for p in range(slots):
        lanes = slice(p * STRIP, (p + 1) * STRIP)
        for half in range(2):
            rows = slice(half * 8, half * 8 + 8)
            lines = [
                jnp.concatenate([y_low[q, rows, lanes], prim_ref[p, q, rows, :], y_high[q, rows, lanes]], axis=1)
                for q in range(FIELDS)
            ]
            for q, value in enumerate(sweep(lines, 1, lane_at)):
                change_ref[p, q, rows, :] += value[:, STRIP : STRIP + PLANE]
    for half in range(2):
        lanes = slice(half * 128, half * 128 + 128)
        lines = [
            jnp.concatenate(
                [x_low[q, :, lanes]] + [prim_ref[p, q, :, lanes] for p in range(slots)] + [x_high[q, :, lanes]], axis=0
            )
            for q in range(FIELDS)
        ]
        for q, value in enumerate(sweep(lines, 0, row_at)):
            for p in range(slots):
                first = GHOST + p * EDGE
                total = change_ref[p, q, :, lanes] + value[first : first + EDGE]
                out_ref[p, q, :, lanes] = u_ref[p, q, :, lanes] - STEP_RATIO * total


def place_kernel(index_ref, owner_ref, slot_ref, own_ref, partner_ref, out_ref):
    slots = own_ref.shape[0]
    me, group_place = index_ref[0], index_ref[1]
    first = (group_place // 2) * (2 * slots)
    low = group_place % 2 == 0
    out_ref[...] = jnp.zeros_like(out_ref)
    for member in range(2):
        for p in range(slots):
            k = first + member * slots + p
            owned = owner_ref[k] == me
            slot = jnp.where(owned, slot_ref[k], 0)
            mine = low if member == 0 else jnp.logical_not(low)

            @pl.when(jnp.logical_and(owned, mine))
            def _(slot=slot, p=p):
                out_ref[slot] = own_ref[p]

            @pl.when(jnp.logical_and(owned, jnp.logical_not(mine)))
            def _(slot=slot, p=p):
                out_ref[slot] = partner_ref[p]


def on_device(patches, new_owner, new_slot):
    slots = patches.shape[0]
    f32 = jnp.float32
    shape = jax.ShapeDtypeStruct
    block = shape((slots, FIELDS, EDGE, PLANE), f32)
    x_side = shape((FIELDS, GHOST, PLANE), f32)
    side = shape((FIELDS, EDGE, slots * STRIP), f32)
    prim, prim_z, x_up, x_down, y_up, y_down, z_up, z_down = pl.pallas_call(
        pack_kernel,
        out_shape=[block, block, x_side, x_side, side, side, side, side],
        in_specs=[VMEM],
        out_specs=[VMEM] * 8,
        name="pack",
    )(patches)

    def shift(value, axis, step):
        count = lax.axis_size(axis)
        return lax.ppermute(value, axis, [(i, (i + step) % count) for i in range(count)])

    z_low, z_high = shift(z_up, "gz", 1), shift(z_down, "gz", -1)
    y_low, y_high = shift(y_up, "gy", 1), shift(y_down, "gy", -1)
    x_low, x_high = shift(x_up, "gx", 1), shift(x_down, "gx", -1)
    advanced = pl.pallas_call(
        update_kernel,
        out_shape=block,
        in_specs=[VMEM] * 9,
        out_specs=VMEM,
        scratch_shapes=[pltpu.VMEM((slots, FIELDS, EDGE, PLANE), f32)],
        name="update",
    )(patches, prim, prim_z, x_low, x_high, y_low, y_high, z_low, z_high)
    members = lax.axis_size("gz")
    partner = lax.ppermute(advanced, "gz", [(i, i ^ 1) for i in range(members)])
    place = lax.axis_index("gz")
    me = (lax.axis_index("gx") * lax.axis_size("gy") + lax.axis_index("gy")) * members + place
    return pl.pallas_call(
        place_kernel,
        out_shape=shape((CAP, FIELDS, EDGE, PLANE), f32),
        in_specs=[SMEM, SMEM, SMEM, VMEM, VMEM],
        out_specs=VMEM,
        name="place",
    )(jnp.stack([me, place]).astype(jnp.int32), new_owner, new_slot, advanced, partner)


def solution(mesh):
    in_specs = (P(("gx", "gy", "gz"), None, None, None), P(("gx", "gy")), P(("gx", "gy")))
    out_specs = P(("gx", "gy", "gz"), None, None, None)
    return jax.shard_map(
        on_device, mesh=mesh, in_specs=in_specs, out_specs=out_specs, check_vma=False
    )
```

time: 142 us -> 45.5 us (0.32)
  the two profiles are of different devices: /device:TPU:1 before, /device:TPU:25 now
where the time goes in v1:
time: 45.5 us; the launch traced here: 45.2 us
  starting transfers between devices  25 us (55%)
  Pallas kernels  13.4 us (29%)
  waiting for transfers between devices  4.75 us (10%)
  local copies, waits for them, and re-layouts  1.31 us (3%)
  other arithmetic  0.58 us (1%)
    ppermute x6, starting transfers between devices, shift(): lax.ppermute(value, axis, [(i, (i + step) % count) for i in range(count)])  16.3 us
    pallas_call x1, Pallas kernels, on_device(): pl.pallas_call(update_kernel, out_shape=block, in_specs=[VMEM] * 9, out_s...  9.64 us
    ppermute x1, starting transfers between devices, on_device(): partner = lax.ppermute(advanced, 'gz', [(i, i ^ 1) for i in range(members)])  8.71 us
    ppermute x6, waiting for transfers between devices, shift(): lax.ppermute(value, axis, [(i, (i + step) % count) for i in range(count)])  4.08 us
    pallas_call x1, Pallas kernels, on_device(): pl.pallas_call(pack_kernel, out_shape=[block, block, x_side, x_side, side...  1.92 us
    pallas_call x1, Pallas kernels, on_device(): pl.pallas_call(place_kernel, out_shape=shape((CAP, FIELDS, EDGE, PLANE),...  1.87 us
    unnamed x14, local copies, waits for them, and re-layouts  1.31 us
  transfers between devices with their start and end apart: 7, of which 2 were waited for; matrix products, arithmetic and copies ran while one was open for 1% of the time, Pallas kernels for 0%

profile of v1, /device:TPU:25, one launch (start us, length us, event | category | flops | bytes accessed | tf_op | source)
XLA Modules:
  0.0 45.2 jit_solution(10194176986220313271)
XLA Ops:
  0.0 1.9 %pack.1 = (f32[2,6,16,256]{3,2,1,0:T(8,128)}, f32[2,6,16,256]{3,2,1,0:T(8,128)}, f32[6,4,256]{2,1,0:T(4,128)}, f32[6,4,256]{2,1,0:T(4,128)}, f32[6,16,128]{2,1,0...) custom-call(f32[2,6,16,256]{3,2,1,0:T(8,128)} %u_ref.3), custom_call_target="tpu_custom_call" | custom-call | tf_op jit(solution)/shard_map/pack/pallas_call | solution.py:183
  1.9 3.1 %collective-permute-start.2 = (f32[6,16,128]{2,1,0:T(8,128)}, f32[6,16,128]{2,1,0:T(8,128)S(1)}, u32[]{:S(2)}, u32[]{:S(2)}) collective-permute-start(f32[6,16,128]{2,1,0:T(8,128)} %get-tuple-element.17), channel_id=1, source_target_pairs={{0,16},{16,32},{32,48},{48,0},{1,17},{17,33},{33,49},{49,1},{2,18}... | collective-permute-start | bytes 147464 | tf_op jit(solution)/shard_map/ppermute | solution.py:193
  5.0 4.4 %collective-permute-start = (f32[6,4,256]{2,1,0:T(4,128)}, f32[6,4,256]{2,1,0:T(4,128)S(1)}, u32[]{:S(2)}, u32[]{:S(2)}) collective-permute-start(f32[6,4,256]{2,1,0:T(4,128)} %get-tuple-element.15), channel_id=1, source_target_pairs={{0,64},{64,128},{128,192},{192,256},{256,320},{320,384},{384,448},... | collective-permute-start | bytes 73736 | tf_op jit(solution)/shard_map/ppermute | solution.py:193
  9.5 3.4 %collective-permute-start.3 = (f32[6,16,128]{2,1,0:T(8,128)}, f32[6,16,128]{2,1,0:T(8,128)S(1)}, u32[]{:S(2)}, u32[]{:S(2)}) collective-permute-start(f32[6,16,128]{2,1,0:T(8,128)} %get-tuple-element.18), channel_id=1, source_target_pairs={{0,48},{16,0},{32,16},{48,32},{1,49},{17,1},{33,17},{49,33},{2,50}... | collective-permute-start | bytes 147464 | tf_op jit(solution)/shard_map/ppermute | solution.py:193
  12.8 3.5 %collective-permute-start.4 = (f32[6,16,128]{2,1,0:T(8,128)}, f32[6,16,128]{2,1,0:T(8,128)S(1)}, u32[]{:S(2)}, u32[]{:S(2)}) collective-permute-start(f32[6,16,128]{2,1,0:T(8,128)} %get-tuple-element.19), channel_id=1, source_target_pairs={{0,1},{1,2},{2,3},{3,4},{4,5},{5,6},{6,7},{7,8},{8,9},{9,10},{10,1... | collective-permute-start | bytes 147464 | tf_op jit(solution)/shard_map/ppermute | solution.py:193
  16.4 0.0 collective-permute-start.5
  16.4 0.0 collective-permute-done.x_low
  16.4 1.9 %collective-permute-start.1 = (f32[6,4,256]{2,1,0:T(4,128)}, f32[6,4,256]{2,1,0:T(4,128)S(1)}, u32[]{:S(2)}, u32[]{:S(2)}) collective-permute-start(f32[6,4,256]{2,1,0:T(4,128)} %get-tuple-element.16), channel_id=1, source_target_pairs={{0,448},{64,0},{128,64},{192,128},{256,192},{320,256},{384,320},{4... | collective-permute-start | bytes 73736 | tf_op jit(solution)/shard_map/ppermute | solution.py:193
  18.3 4.1 %collective-permute-done.1.x_high = f32[6,4,256]{2,1,0:T(4,128)S(1)} collective-permute-done((f32[6,4,256]{2,1,0:T(4,128)}, f32[6,4,256]{2,1,0:T(4,128)S(1)}, u32[]{:S(2)}, u32[]{:S(2)}) %collective-permute-start.1) | collective-permute-done | bytes 24608 | tf_op jit(solution)/shard_map/ppermute | solution.py:193
  22.4 0.0 collective-permute-done.2.y_low
  22.4 0.0 collective-permute-done.3.y_high
  22.4 0.0 collective-permute-done.4.z_low
  22.4 0.0 collective-permute-done.5.z_high
  22.4 0.5 %copy-done.6 = f32[6,4,256]{2,1,0:T(4,128)} copy-done((f32[6,4,256]{2,1,0:T(4,128)}, f32[6,4,256]{2,1,0:T(4,128)S(1)}, u32[]{:S(2)}) %copy-start.6) | copy-done | bytes 24600
  23.0 0.0 copy-done.1
  23.0 0.0 copy-done.2
  23.0 0.0 copy-done.3
  23.0 0.0 copy-done.4
  23.0 9.6 %update.1.own_ref = f32[2,6,16,256]{3,2,1,0:T(8,128)} custom-call(f32[2,6,16,256]{3,2,1,0:T(8,128)} %u_ref.3, f32[2,6,16,256]{3,2,1,0:T(8,128)} %get-tuple-element.13.prim_ref, f32[2,6,16,256]{3,2,1,0:T(8,128)} %get-tuple-element.14.prim_z_ref, f32[6,4,256]{2,1,0:T(4,128)} %copy-done.5, f32[6,4,256]{2,1,0:T(4,128)} %copy-done.6, f32[6,16,128]{2,1,0:T(8,128)} %copy-done.1, ...), custom_call_target="tpu_custom_call" | custom-call | tf_op jit(solution)/shard_map/update/pallas_call | solution.py:198
  32.7 8.7 %collective-permute-start.6 = (f32[2,6,16,256]{3,2,1,0:T(8,128)}, f32[2,6,16,256]{3,2,1,0:T(8,128)S(1)}, u32[]{:S(2)}, u32[]{:S(2)}) collective-permute-start(f32[2,6,16,256]{3,2,1,0:T(8,128)} %update.1.own_ref), channel_id=1, source_target_pairs={{0,1},{1,0},{2,3},{3,2},{4,5},{5,4},{6,7},{7,6},{8,9},{9,8},{10,11... | collective-permute-start | bytes 589832 | tf_op jit(solution)/shard_map/ppermute | solution.py:207
  41.4 0.6 %pad_add_fusion.index_ref = s32[2]{0:T(128)} fusion(s32[1]{0:T(128)} %bitcast.1, s32[1]{0:T(128)} %bitcast), kind=kLoop, calls=%fused_computation | loop fusion | flops 2 | bytes 16 | tf_op jit(solution)/shard_map/stack | solution.py:216
  42.0 0.7 %collective-permute-done.6.partner_ref = f32[2,6,16,256]{3,2,1,0:T(8,128)S(1)} collective-permute-done((f32[2,6,16,256]{3,2,1,0:T(8,128)}, f32[2,6,16,256]{3,2,1,0:T(8,128)S(1)}, u32[]{:S(2)}, u32[]{:S(2)}) %collective-permute-start.6) | collective-permute-done | bytes 196640 | tf_op jit(solution)/shard_map/ppermute | solution.py:207
  42.7 0.7 %copy-done = f32[2,6,16,256]{3,2,1,0:T(8,128)} copy-done((f32[2,6,16,256]{3,2,1,0:T(8,128)}, f32[2,6,16,256]{3,2,1,0:T(8,128)S(1)}, u32[]{:S(2)}) %copy-start) | copy-done | bytes 196632
  43.3 1.9 %place.1 = f32[4,6,16,256]{3,2,1,0:T(8,128)} custom-call(s32[2]{0:T(128)} %pad_add_fusion.index_ref, s32[32]{0:T(128)} %owner_ref.1, s32[32]{0:T(128)} %slot_ref.1, f32[2,6,16,256]{3,2,1,0:T(8,128)} %update.1.own_ref, f32[2,6,16,256]{3,2,1,0:T(8,128)} %copy-done), custom_call_target="tpu_custom_call" | custom-call | tf_op jit(solution)/shard_map/place/pallas_call | solution.py:210
  (8 shorter events, 0.0 us)
Async XLA Ops:
  1.9 20.4 %collective-permute-start.2 = (f32[6,16,128]{2,1,0:T(8,128)}, f32[6,16,128]{2,1,0:T(8,128)S(1)}, u32[]{:S(2)}, u32[]{:S(2)}) collective-permute-start(f32[6,16,128]{2,1,0:T(8,128)} %get-tuple-element.17), channel_id=1, source_target_pairs={{0,16},{16,32},{32,48},{48,0},{1,17},{17,33},{33,49},{49,1},{2,18}... | collective-permute-start | bytes 147464 | tf_op jit(solution)/shard_map/ppermute | solution.py:193
  5.0 11.3 %collective-permute-start = (f32[6,4,256]{2,1,0:T(4,128)}, f32[6,4,256]{2,1,0:T(4,128)S(1)}, u32[]{:S(2)}, u32[]{:S(2)}) collective-permute-start(f32[6,4,256]{2,1,0:T(4,128)} %get-tuple-element.15), channel_id=1, source_target_pairs={{0,64},{64,128},{128,192},{192,256},{256,320},{320,384},{384,448},... | collective-permute-start | bytes 73736 | tf_op jit(solution)/shard_map/ppermute | solution.py:193
  9.5 12.9 %collective-permute-start.3 = (f32[6,16,128]{2,1,0:T(8,128)}, f32[6,16,128]{2,1,0:T(8,128)S(1)}, u32[]{:S(2)}, u32[]{:S(2)}) collective-permute-start(f32[6,16,128]{2,1,0:T(8,128)} %get-tuple-element.18), channel_id=1, source_target_pairs={{0,48},{16,0},{32,16},{48,32},{1,49},{17,1},{33,17},{49,33},{2,50}... | collective-permute-start | bytes 147464 | tf_op jit(solution)/shard_map/ppermute | solution.py:193
  12.8 9.5 %collective-permute-start.4 = (f32[6,16,128]{2,1,0:T(8,128)}, f32[6,16,128]{2,1,0:T(8,128)S(1)}, u32[]{:S(2)}, u32[]{:S(2)}) collective-permute-start(f32[6,16,128]{2,1,0:T(8,128)} %get-tuple-element.19), channel_id=1, source_target_pairs={{0,1},{1,2},{2,3},{3,4},{4,5},{5,6},{6,7},{7,8},{8,9},{9,10},{10,1... | collective-permute-start | bytes 147464 | tf_op jit(solution)/shard_map/ppermute | solution.py:193
  16.4 6.0 %collective-permute-start.5 = (f32[6,16,128]{2,1,0:T(8,128)}, f32[6,16,128]{2,1,0:T(8,128)S(1)}, u32[]{:S(2)}, u32[]{:S(2)}) collective-permute-start(f32[6,16,128]{2,1,0:T(8,128)} %get-tuple-element.20), channel_id=1, source_target_pairs={{0,15},{1,0},{2,1},{3,2},{4,3},{5,4},{6,5},{7,6},{8,7},{9,8},{10,9... | collective-permute-start | bytes 147464 | tf_op jit(solution)/shard_map/ppermute | solution.py:193
  16.4 6.1 %copy-start.5 = (f32[6,4,256]{2,1,0:T(4,128)}, f32[6,4,256]{2,1,0:T(4,128)S(1)}, u32[]{:S(2)}) copy-start(f32[6,4,256]{2,1,0:T(4,128)S(1)} %collective-permute-done.x_low) | copy-start | bytes 73732
  16.4 6.0 %collective-permute-start.1 = (f32[6,4,256]{2,1,0:T(4,128)}, f32[6,4,256]{2,1,0:T(4,128)S(1)}, u32[]{:S(2)}, u32[]{:S(2)}) collective-permute-start(f32[6,4,256]{2,1,0:T(4,128)} %get-tuple-element.16), channel_id=1, source_target_pairs={{0,448},{64,0},{128,64},{192,128},{256,192},{320,256},{384,320},{4... | collective-permute-start | bytes 73736 | tf_op jit(solution)/shard_map/ppermute | solution.py:193
  22.4 0.6 %copy-start.6 = (f32[6,4,256]{2,1,0:T(4,128)}, f32[6,4,256]{2,1,0:T(4,128)S(1)}, u32[]{:S(2)}) copy-start(f32[6,4,256]{2,1,0:T(4,128)S(1)} %collective-permute-done.1.x_high) | copy-start | bytes 73732
  22.4 0.6 %copy-start.1 = (f32[6,16,128]{2,1,0:T(8,128)}, f32[6,16,128]{2,1,0:T(8,128)S(1)}, u32[]{:S(2)}) copy-start(f32[6,16,128]{2,1,0:T(8,128)S(1)} %collective-permute-done.2.y_low) | copy-start | bytes 147460
  22.4 0.6 %copy-start.2 = (f32[6,16,128]{2,1,0:T(8,128)}, f32[6,16,128]{2,1,0:T(8,128)S(1)}, u32[]{:S(2)}) copy-start(f32[6,16,128]{2,1,0:T(8,128)S(1)} %collective-permute-done.3.y_high) | copy-start | bytes 147460
  22.4 0.6 %copy-start.3 = (f32[6,16,128]{2,1,0:T(8,128)}, f32[6,16,128]{2,1,0:T(8,128)S(1)}, u32[]{:S(2)}) copy-start(f32[6,16,128]{2,1,0:T(8,128)S(1)} %collective-permute-done.4.z_low) | copy-start | bytes 147460
  22.4 0.6 %copy-start.4 = (f32[6,16,128]{2,1,0:T(8,128)}, f32[6,16,128]{2,1,0:T(8,128)S(1)}, u32[]{:S(2)}) copy-start(f32[6,16,128]{2,1,0:T(8,128)S(1)} %collective-permute-done.5.z_high) | copy-start | bytes 147460
  32.7 10.0 %collective-permute-start.6 = (f32[2,6,16,256]{3,2,1,0:T(8,128)}, f32[2,6,16,256]{3,2,1,0:T(8,128)S(1)}, u32[]{:S(2)}, u32[]{:S(2)}) collective-permute-start(f32[2,6,16,256]{3,2,1,0:T(8,128)} %update.1.own_ref), channel_id=1, source_target_pairs={{0,1},{1,0},{2,3},{3,2},{4,5},{5,4},{6,7},{7,6},{8,9},{9,8},{10,11... | collective-permute-start | bytes 589832 | tf_op jit(solution)/shard_map/ppermute | solution.py:207
  42.7 0.7 %copy-start = (f32[2,6,16,256]{3,2,1,0:T(8,128)}, f32[2,6,16,256]{3,2,1,0:T(8,128)S(1)}, u32[]{:S(2)}) copy-start(f32[2,6,16,256]{3,2,1,0:T(8,128)S(1)} %collective-permute-done.6.partner_ref) | copy-start | bytes 589828

commit v2 on v1

--- a/solution.py
+++ b/solution.py
@@ -1,5 +1,3 @@
-import functools
-
 import jax
 import jax.numpy as jnp
 from jax import lax
@@ -13,9 +11,11 @@
 FIELDS = 6
 PLANE = EDGE * EDGE
 STRIP = GHOST * EDGE
+HALF = 128
 
 STEP_RATIO = 0.08
 VMEM = pl.BlockSpec(memory_space=pltpu.VMEM)
+ANY = pl.BlockSpec(memory_space=pl.ANY)
 SMEM = pl.BlockSpec(memory_space=pltpu.SMEM)
 
 
@@ -85,26 +85,49 @@
     return total
 
 
-def pack_kernel(u_ref, prim_ref, prim_z_ref, x_up, x_down, y_up, y_down, z_up, z_down):
+def to_lines(first, second):
+    left = lax.broadcasted_iota(jnp.int32, (2 * EDGE, HALF), 1) < STRIP
+    rows = []
+    for part in range(2):
+        one = first.reshape(2 * EDGE, PLANE)[:, part * HALF : (part + 1) * HALF]
+        two = second.reshape(2 * EDGE, PLANE)[:, part * HALF : (part + 1) * HALF]
+        rows.append(jnp.where(left, one, pltpu.roll(two, STRIP, 1)))
+        rows.append(jnp.where(left, pltpu.roll(one, STRIP, 1), two))
+    lines = jnp.concatenate(rows, axis=0).T
+    return lines[:STRIP], lines[STRIP:]
+
+
+def from_lines(first, second):
+    left = lax.broadcasted_iota(jnp.int32, (2 * EDGE, HALF), 1) < STRIP
+    rows = jnp.concatenate([first, second], axis=0).T
+    rows = [rows[k * 2 * EDGE : (k + 1) * 2 * EDGE] for k in range(4)]
+    one, two = [], []
+    for part in range(2):
+        low, high = rows[2 * part], rows[2 * part + 1]
+        one.append(jnp.where(left, low, pltpu.roll(high, STRIP, 1)))
+        two.append(jnp.where(left, pltpu.roll(low, STRIP, 1), high))
+    return jnp.concatenate(one, axis=1), jnp.concatenate(two, axis=1)
+
+
+def pack_kernel(u_ref, prim_ref, lines_z, lines_y, x_up, x_down, y_up, y_down, z_up, z_down):
     slots = u_ref.shape[0]
     for p in range(slots):
         for q, value in enumerate(to_primitive([u_ref[p, q] for q in range(FIELDS)])):
             prim_ref[p, q] = value
-    flat = prim_ref[...].reshape(slots * FIELDS * EDGE, PLANE)
-    prim_z_ref[...] = exchange_lanes(flat).reshape(slots, FIELDS, EDGE, PLANE)
     x_up[...] = prim_ref[slots - 1, :, EDGE - GHOST :, :]
     x_down[...] = prim_ref[0, :, :GHOST, :]
-    for p in range(slots):
-        lanes = slice(p * STRIP, (p + 1) * STRIP)
-        y_up[:, :, lanes] = prim_ref[p, :, :, PLANE - STRIP :]
-        y_down[:, :, lanes] = prim_ref[p, :, :, :STRIP]
-        z_up[:, :, lanes] = prim_z_ref[p, :, :, PLANE - STRIP :]
-        z_down[:, :, lanes] = prim_z_ref[p, :, :, :STRIP]
-
-
-def lane_at(value, k):
-    width = value.shape[1]
-    return pltpu.roll(value, (-k * EDGE) % width, 1)
+    swapped = exchange_lanes(prim_ref[...].reshape(slots * FIELDS * EDGE, PLANE))
+    swapped = swapped.reshape(slots, FIELDS, EDGE, PLANE)
+    for pair in range(0, FIELDS, 2):
+        for ref, pieces in (
+            (lines_z, to_lines(prim_ref[:, pair], prim_ref[:, pair + 1])),
+            (lines_y, to_lines(swapped[:, pair], swapped[:, pair + 1])),
+        ):
+            for k in range(2):
+                ref[pair + k] = pieces[k].reshape(GHOST, EDGE, HALF)
+    for ref, up, down in ((lines_z, z_up, z_down), (lines_y, y_up, y_down)):
+        up[...] = ref[:, :, EDGE - GHOST :, :]
+        down[...] = ref[:, :, :GHOST, :]
 
 
 def row_at(value, k):
@@ -112,32 +135,35 @@
     return pltpu.roll(value, (-k) % height, 0)
 
 
-def update_kernel(u_ref, prim_ref, prim_z_ref, x_low, x_high, y_low, y_high, z_low, z_high, out_ref, change_ref):
+def sweep_lines(low, lines, high, normal, change):
+    for group in range(GHOST):
+        extended = [
+            jnp.concatenate([low[q, group], lines[q, group], high[q, group]], axis=0) for q in range(FIELDS)
+        ]
+        for q, value in enumerate(sweep(extended, normal, row_at)):
+            change[q, group] = value[GHOST : GHOST + EDGE]
+
+
+def lines_kernel(lines_z, lines_y, z_low, z_high, y_low, y_high, out_ref, change_z, change_y):
+    slots = out_ref.shape[0]
+    sweep_lines(y_low, lines_y, y_high, 1, change_y)
+    for pair in range(0, FIELDS, 2):
+        parts = from_lines(change_y[pair].reshape(STRIP, HALF), change_y[pair + 1].reshape(STRIP, HALF))
+        for k in range(2):
+            out_ref[:, pair + k] = parts[k].reshape(slots, EDGE, PLANE)
+    flat = out_ref[...].reshape(slots * FIELDS * EDGE, PLANE)
+    out_ref[...] = exchange_lanes(flat).reshape(slots, FIELDS, EDGE, PLANE)
+    sweep_lines(z_low, lines_z, z_high, 2, change_z)
+    for pair in range(0, FIELDS, 2):
+        parts = from_lines(change_z[pair].reshape(STRIP, HALF), change_z[pair + 1].reshape(STRIP, HALF))
+        for k in range(2):
+            out_ref[:, pair + k] += parts[k].reshape(slots, EDGE, PLANE)
+
+
+def finish_kernel(u_ref, prim_ref, change_ref, x_low, x_high, out_ref):
     slots = u_ref.shape[0]
-    for p in range(slots):
-        lanes = slice(p * STRIP, (p + 1) * STRIP)
-        for half in range(2):
-            rows = slice(half * 8, half * 8 + 8)
-            lines = [
-                jnp.concatenate([z_low[q, rows, lanes], prim_z_ref[p, q, rows, :], z_high[q, rows, lanes]], axis=1)
-                for q in range(FIELDS)
-            ]
-            for q, value in enumerate(sweep(lines, 2, lane_at)):
-                change_ref[p, q, rows, :] = value[:, STRIP : STRIP + PLANE]
-    flat = change_ref[...].reshape(slots * FIELDS * EDGE, PLANE)
-    change_ref[...] = exchange_lanes(flat).reshape(slots, FIELDS, EDGE, PLANE)
-    for p in range(slots):
-        lanes = slice(p * STRIP, (p + 1) * STRIP)
-        for half in range(2):
-            rows = slice(half * 8, half * 8 + 8)
-            lines = [
-                jnp.concatenate([y_low[q, rows, lanes], prim_ref[p, q, rows, :], y_high[q, rows, lanes]], axis=1)
-                for q in range(FIELDS)
-            ]
-            for q, value in enumerate(sweep(lines, 1, lane_at)):
-                change_ref[p, q, rows, :] += value[:, STRIP : STRIP + PLANE]
     for half in range(2):
-        lanes = slice(half * 128, half * 128 + 128)
+        lanes = slice(half * HALF, half * HALF + HALF)
         lines = [
             jnp.concatenate(
                 [x_low[q, :, lanes]] + [prim_ref[p, q, :, lanes] for p in range(slots)] + [x_high[q, :, lanes]], axis=0
@@ -151,26 +177,31 @@
                 out_ref[p, q, :, lanes] = u_ref[p, q, :, lanes] - STEP_RATIO * total
 
 
-def place_kernel(index_ref, owner_ref, slot_ref, own_ref, partner_ref, out_ref):
+def place_kernel(index_ref, owner_ref, slot_ref, own_ref, partner_ref, out_ref, zeros, sems):
     slots = own_ref.shape[0]
     me, group_place = index_ref[0], index_ref[1]
     first = (group_place // 2) * (2 * slots)
-    low = group_place % 2 == 0
-    out_ref[...] = jnp.zeros_like(out_ref)
-    for member in range(2):
-        for p in range(slots):
-            k = first + member * slots + p
-            owned = owner_ref[k] == me
-            slot = jnp.where(owned, slot_ref[k], 0)
-            mine = low if member == 0 else jnp.logical_not(low)
-
-            @pl.when(jnp.logical_and(owned, mine))
-            def _(slot=slot, p=p):
-                out_ref[slot] = own_ref[p]
-
-            @pl.when(jnp.logical_and(owned, jnp.logical_not(mine)))
-            def _(slot=slot, p=p):
-                out_ref[slot] = partner_ref[p]
+    side = group_place % 2
+    zeros[...] = jnp.zeros_like(zeros)
+    for s in range(CAP):
+        empty = True
+        for member in range(2):
+            for p in range(slots):
+                k = first + member * slots + p
+                here = jnp.logical_and(owner_ref[k] == me, slot_ref[k] == s)
+                empty = jnp.logical_and(empty, jnp.logical_not(here))
+                for ref, wanted in ((own_ref, side == member), (partner_ref, side != member)):
+
+                    @pl.when(jnp.logical_and(here, wanted))
+                    def _(ref=ref, p=p, s=s):
+                        pltpu.make_async_copy(ref.at[p], out_ref.at[s], sems.at[s]).start()
+
+        @pl.when(empty)
+        def _(s=s):
+            pltpu.make_async_copy(zeros, out_ref.at[s], sems.at[s]).start()
+
+    for s in range(CAP):
+        pltpu.make_async_copy(zeros, out_ref.at[s], sems.at[s]).wait()
 
 
 def on_device(patches, new_owner, new_slot):
@@ -178,13 +209,14 @@
     f32 = jnp.float32
     shape = jax.ShapeDtypeStruct
     block = shape((slots, FIELDS, EDGE, PLANE), f32)
+    lines = shape((FIELDS, GHOST, EDGE, HALF), f32)
     x_side = shape((FIELDS, GHOST, PLANE), f32)
-    side = shape((FIELDS, EDGE, slots * STRIP), f32)
-    prim, prim_z, x_up, x_down, y_up, y_down, z_up, z_down = pl.pallas_call(
+    side = shape((FIELDS, GHOST, GHOST, HALF), f32)
+    prim, lines_z, lines_y, x_up, x_down, y_up, y_down, z_up, z_down = pl.pallas_call(
         pack_kernel,
-        out_shape=[block, block, x_side, x_side, side, side, side, side],
+        out_shape=[block, lines, lines, x_side, x_side, side, side, side, side],
         in_specs=[VMEM],
-        out_specs=[VMEM] * 8,
+        out_specs=[VMEM] * 9,
         name="pack",
     )(patches)
 
@@ -195,14 +227,17 @@
     z_low, z_high = shift(z_up, "gz", 1), shift(z_down, "gz", -1)
     y_low, y_high = shift(y_up, "gy", 1), shift(y_down, "gy", -1)
     x_low, x_high = shift(x_up, "gx", 1), shift(x_down, "gx", -1)
+    change = pl.pallas_call(
+        lines_kernel,
+        out_shape=block,
+        in_specs=[VMEM] * 6,
+        out_specs=VMEM,
+        scratch_shapes=[pltpu.VMEM(lines.shape, f32)] * 2,
+        name="lines",
+    )(lines_z, lines_y, z_low, z_high, y_low, y_high)
     advanced = pl.pallas_call(
-        update_kernel,
-        out_shape=block,
-        in_specs=[VMEM] * 9,
-        out_specs=VMEM,
-        scratch_shapes=[pltpu.VMEM((slots, FIELDS, EDGE, PLANE), f32)],
-        name="update",
-    )(patches, prim, prim_z, x_low, x_high, y_low, y_high, z_low, z_high)
+        finish_kernel, out_shape=block, in_specs=[VMEM] * 5, out_specs=VMEM, name="finish"
+    )(patches, prim, change, x_low, x_high)
     members = lax.axis_size("gz")
     partner = lax.ppermute(advanced, "gz", [(i, i ^ 1) for i in range(members)])
     place = lax.axis_index("gz")
@@ -210,8 +245,9 @@
     return pl.pallas_call(
         place_kernel,
         out_shape=shape((CAP, FIELDS, EDGE, PLANE), f32),
-        in_specs=[SMEM, SMEM, SMEM, VMEM, VMEM],
-        out_specs=VMEM,
+        in_specs=[SMEM, SMEM, SMEM, ANY, ANY],
+        out_specs=ANY,
+        scratch_shapes=[pltpu.VMEM((FIELDS, EDGE, PLANE), f32), pltpu.SemaphoreType.DMA((CAP,))],
         name="place",
     )(jnp.stack([me, place]).astype(jnp.int32), new_owner, new_slot, advanced, partner)
 

time: 45.5 us -> 49.6 us (1.090)
  the two profiles are of different devices: /device:TPU:25 before, /device:TPU:30 now
where the time goes in v2:
time: 49.6 us; the launch traced here: 49.3 us
  starting transfers between devices  22.8 us (46%)
  Pallas kernels  21.4 us (43%)
  waiting for transfers between devices  2.41 us (5%)
  local copies, waits for them, and re-layouts  1.9 us (4%)
  other arithmetic  0.58 us (1%)
    ppermute x6, starting transfers between devices, shift(): lax.ppermute(value, axis, [(i, (i + step) % count) for i in range(count)])  20.9 us
    pallas_call x1, Pallas kernels, on_device(): pl.pallas_call(place_kernel, out_shape=shape((CAP, FIELDS, EDGE, PLANE),...  13.7 us
    pallas_call x1, Pallas kernels, on_device(): pl.pallas_call(lines_kernel, out_shape=block, in_specs=[VMEM] * 6, out_sp...  3.17 us
    pallas_call x1, Pallas kernels, on_device(): pl.pallas_call(finish_kernel, out_shape=block, in_specs=[VMEM] * 5, out_s...  2.32 us
    pallas_call x1, Pallas kernels, on_device(): pl.pallas_call(pack_kernel, out_shape=[block, lines, lines, x_side, x_sid...  2.19 us
    ppermute x1, starting transfers between devices, on_device(): partner = lax.ppermute(advanced, 'gz', [(i, i ^ 1) for i in range(members)])  1.91 us
    unnamed x14, local copies, waits for them, and re-layouts  1.9 us
    ppermute x6, waiting for transfers between devices, shift(): lax.ppermute(value, axis, [(i, (i + step) % count) for i in range(count)])  1.37 us
  transfers between devices with their start and end apart: 7, of which 2 were waited for; matrix products, arithmetic and copies ran while one was open for 1% of the time, Pallas kernels for 6%

profile of v2, /device:TPU:30, one launch (start us, length us, event | category | flops | bytes accessed | tf_op | source)
XLA Modules:
  0.0 49.3 jit_solution(11557677298592101829)
XLA Ops:
  0.0 2.2 %pack.1 = (f32[2,6,16,256]{3,2,1,0:T(8,128)}, f32[6,4,16,128]{3,2,1,0:T(8,128)}, f32[6,4,16,128]{3,2,1,0:T(8,128)}, f32[6,4,256]{2,1,0:T(4,128)}, f32[6,4,256]{2...) custom-call(f32[2,6,16,256]{3,2,1,0:T(8,128)} %u_ref.3), custom_call_target="tpu_custom_call" | custom-call | tf_op jit(solution)/shard_map/pack/pallas_call | solution.py:215
  2.2 0.0 collective-permute-start
  2.2 8.5 %collective-permute-start.1 = (f32[6,4,4,128]{3,2,1,0:T(4,128)}, f32[6,4,4,128]{3,2,1,0:T(4,128)S(1)}, u32[]{:S(2)}, u32[]{:S(2)}) collective-permute-start(f32[6,4,4,128]{3,2,1,0:T(4,128)} %get-tuple-element.18), channel_id=1, source_target_pairs={{0,15},{1,0},{2,1},{3,2},{4,3},{5,4},{6,5},{7,6},{8,7},{9,8},{10,9... | collective-permute-start | bytes 147464 | tf_op jit(solution)/shard_map/ppermute | solution.py:225
  10.7 2.4 %collective-permute-start.2 = (f32[6,4,4,128]{3,2,1,0:T(4,128)}, f32[6,4,4,128]{3,2,1,0:T(4,128)S(1)}, u32[]{:S(2)}, u32[]{:S(2)}) collective-permute-start(f32[6,4,4,128]{3,2,1,0:T(4,128)} %get-tuple-element.19), channel_id=1, source_target_pairs={{0,16},{16,32},{32,48},{48,0},{1,17},{17,33},{33,49},{49,1},{2,18}... | collective-permute-start | bytes 147464 | tf_op jit(solution)/shard_map/ppermute | solution.py:225
  13.1 3.5 %collective-permute-start.3 = (f32[6,4,4,128]{3,2,1,0:T(4,128)}, f32[6,4,4,128]{3,2,1,0:T(4,128)S(1)}, u32[]{:S(2)}, u32[]{:S(2)}) collective-permute-start(f32[6,4,4,128]{3,2,1,0:T(4,128)} %get-tuple-element.20), channel_id=1, source_target_pairs={{0,48},{16,0},{32,16},{48,32},{1,49},{17,1},{33,17},{49,33},{2,50}... | collective-permute-start | bytes 147464 | tf_op jit(solution)/shard_map/ppermute | solution.py:225
  16.5 4.7 %collective-permute-start.4 = (f32[6,4,256]{2,1,0:T(4,128)}, f32[6,4,256]{2,1,0:T(4,128)S(1)}, u32[]{:S(2)}, u32[]{:S(2)}) collective-permute-start(f32[6,4,256]{2,1,0:T(4,128)} %get-tuple-element.21), channel_id=1, source_target_pairs={{0,64},{64,128},{128,192},{192,256},{256,320},{320,384},{384,448},... | collective-permute-start | bytes 73736 | tf_op jit(solution)/shard_map/ppermute | solution.py:225
  21.2 0.0 collective-permute-done.z_low
  21.3 1.9 %collective-permute-start.5 = (f32[6,4,256]{2,1,0:T(4,128)}, f32[6,4,256]{2,1,0:T(4,128)S(1)}, u32[]{:S(2)}, u32[]{:S(2)}) collective-permute-start(f32[6,4,256]{2,1,0:T(4,128)} %get-tuple-element.22), channel_id=1, source_target_pairs={{0,448},{64,0},{128,64},{192,128},{256,192},{320,256},{384,320},{4... | collective-permute-start | bytes 73736 | tf_op jit(solution)/shard_map/ppermute | solution.py:225
  23.2 0.0 collective-permute-done.1.z_high
  23.2 0.0 collective-permute-done.2.y_low
  23.2 0.0 collective-permute-done.3.y_high
  23.2 0.6 %copy-done.2 = f32[6,4,4,128]{3,2,1,0:T(4,128)} copy-done((f32[6,4,4,128]{3,2,1,0:T(4,128)}, f32[6,4,4,128]{3,2,1,0:T(4,128)S(1)}, u32[]{:S(2)}) %copy-start.2) | copy-done | bytes 49176
  23.8 0.0 copy-done.3
  23.8 0.0 copy-done.4
  23.9 3.2 %lines.1.change_ref = f32[2,6,16,256]{3,2,1,0:T(8,128)} custom-call(f32[6,4,16,128]{3,2,1,0:T(8,128)} %get-tuple-element.15.lines_z, f32[6,4,16,128]{3,2,1,0:T(8,128)} %get-tuple-element.16.lines_y, f32[6,4,4,128]{3,2,1,0:T(4,128)} %copy-done.1, f32[6,4,4,128]{3,2,1,0:T(4,128)} %copy-done.2, f32[6,4,4,128]{3,2,1,0:T(4,128)} %copy-done.3, ...), custom_call_target="tpu_custom_call" | custom-call | tf_op jit(solution)/shard_map/lines/pallas_call | solution.py:230
  27.0 0.0 collective-permute-done.4.x_low
  27.0 1.4 %collective-permute-done.5.x_high = f32[6,4,256]{2,1,0:T(4,128)S(1)} collective-permute-done((f32[6,4,256]{2,1,0:T(4,128)}, f32[6,4,256]{2,1,0:T(4,128)S(1)}, u32[]{:S(2)}, u32[]{:S(2)}) %collective-permute-start.5) | collective-permute-done | bytes 24608 | tf_op jit(solution)/shard_map/ppermute | solution.py:225
  28.4 0.6 %copy-done.6 = f32[6,4,256]{2,1,0:T(4,128)} copy-done((f32[6,4,256]{2,1,0:T(4,128)}, f32[6,4,256]{2,1,0:T(4,128)S(1)}, u32[]{:S(2)}) %copy-start.6) | copy-done | bytes 24600
  29.0 2.3 %finish.1.own_ref = f32[2,6,16,256]{3,2,1,0:T(8,128)} custom-call(f32[2,6,16,256]{3,2,1,0:T(8,128)} %u_ref.3, f32[2,6,16,256]{3,2,1,0:T(8,128)} %get-tuple-element.14.prim_ref, f32[2,6,16,256]{3,2,1,0:T(8,128)} %lines.1.change_ref, f32[6,4,256]{2,1,0:T(4,128)} %copy-done.5, f32[6,4,256]{2,1,0:T(4,128)} %copy-done.6), custom_call_target="tpu_custom_call" | custom-call | tf_op jit(solution)/shard_map/finish/pallas_call | solution.py:238
  31.3 1.9 %collective-permute-start.6 = (f32[2,6,16,256]{3,2,1,0:T(8,128)}, f32[2,6,16,256]{3,2,1,0:T(8,128)S(1)}, u32[]{:S(2)}, u32[]{:S(2)}) collective-permute-start(f32[2,6,16,256]{3,2,1,0:T(8,128)} %finish.1.own_ref), channel_id=1, source_target_pairs={{0,1},{1,0},{2,3},{3,2},{4,5},{5,4},{6,7},{7,6},{8,9},{9,8},{10,11... | collective-permute-start | bytes 589832 | tf_op jit(solution)/shard_map/ppermute | solution.py:242
  33.2 0.6 %pad_add_fusion.index_ref = s32[2]{0:T(128)} fusion(s32[1]{0:T(128)} %bitcast.1, s32[1]{0:T(128)} %bitcast), kind=kLoop, calls=%fused_computation | loop fusion | flops 2 | bytes 16 | tf_op jit(solution)/shard_map/stack | solution.py:252
  33.8 1.0 %collective-permute-done.6.partner_ref = f32[2,6,16,256]{3,2,1,0:T(8,128)S(1)} collective-permute-done((f32[2,6,16,256]{3,2,1,0:T(8,128)}, f32[2,6,16,256]{3,2,1,0:T(8,128)S(1)}, u32[]{:S(2)}, u32[]{:S(2)}) %collective-permute-start.6) | collective-permute-done | bytes 196640 | tf_op jit(solution)/shard_map/ppermute | solution.py:242
  34.9 0.7 %copy-done = f32[2,6,16,256]{3,2,1,0:T(8,128)} copy-done((f32[2,6,16,256]{3,2,1,0:T(8,128)}, f32[2,6,16,256]{3,2,1,0:T(8,128)S(1)}, u32[]{:S(2)}) %copy-start) | copy-done | bytes 196632
  35.5 13.7 %place.1 = f32[4,6,16,256]{3,2,1,0:T(8,128)} custom-call(s32[2]{0:T(128)} %pad_add_fusion.index_ref, s32[32]{0:T(128)} %owner_ref.1, s32[32]{0:T(128)} %slot_ref.1, f32[2,6,16,256]{3,2,1,0:T(8,128)} %finish.1.own_ref, f32[2,6,16,256]{3,2,1,0:T(8,128)} %copy-done), custom_call_target="tpu_custom_call" | custom-call | tf_op jit(solution)/shard_map/place/pallas_call | solution.py:245
  (9 shorter events, 0.0 us)
Async XLA Ops:
  2.2 19.0 %collective-permute-start = (f32[6,4,4,128]{3,2,1,0:T(4,128)}, f32[6,4,4,128]{3,2,1,0:T(4,128)S(1)}, u32[]{:S(2)}, u32[]{:S(2)}) collective-permute-start(f32[6,4,4,128]{3,2,1,0:T(4,128)} %get-tuple-element.17), channel_id=1, source_target_pairs={{0,1},{1,2},{2,3},{3,4},{4,5},{5,6},{6,7},{7,8},{8,9},{9,10},{10,1... | collective-permute-start | bytes 147464 | tf_op jit(solution)/shard_map/ppermute | solution.py:225
  2.2 21.0 %collective-permute-start.1 = (f32[6,4,4,128]{3,2,1,0:T(4,128)}, f32[6,4,4,128]{3,2,1,0:T(4,128)S(1)}, u32[]{:S(2)}, u32[]{:S(2)}) collective-permute-start(f32[6,4,4,128]{3,2,1,0:T(4,128)} %get-tuple-element.18), channel_id=1, source_target_pairs={{0,15},{1,0},{2,1},{3,2},{4,3},{5,4},{6,5},{7,6},{8,7},{9,8},{10,9... | collective-permute-start | bytes 147464 | tf_op jit(solution)/shard_map/ppermute | solution.py:225
  10.7 12.5 %collective-permute-start.2 = (f32[6,4,4,128]{3,2,1,0:T(4,128)}, f32[6,4,4,128]{3,2,1,0:T(4,128)S(1)}, u32[]{:S(2)}, u32[]{:S(2)}) collective-permute-start(f32[6,4,4,128]{3,2,1,0:T(4,128)} %get-tuple-element.19), channel_id=1, source_target_pairs={{0,16},{16,32},{32,48},{48,0},{1,17},{17,33},{33,49},{49,1},{2,18}... | collective-permute-start | bytes 147464 | tf_op jit(solution)/shard_map/ppermute | solution.py:225
  13.1 10.2 %collective-permute-start.3 = (f32[6,4,4,128]{3,2,1,0:T(4,128)}, f32[6,4,4,128]{3,2,1,0:T(4,128)S(1)}, u32[]{:S(2)}, u32[]{:S(2)}) collective-permute-start(f32[6,4,4,128]{3,2,1,0:T(4,128)} %get-tuple-element.20), channel_id=1, source_target_pairs={{0,48},{16,0},{32,16},{48,32},{1,49},{17,1},{33,17},{49,33},{2,50}... | collective-permute-start | bytes 147464 | tf_op jit(solution)/shard_map/ppermute | solution.py:225
  16.5 10.5 %collective-permute-start.4 = (f32[6,4,256]{2,1,0:T(4,128)}, f32[6,4,256]{2,1,0:T(4,128)S(1)}, u32[]{:S(2)}, u32[]{:S(2)}) collective-permute-start(f32[6,4,256]{2,1,0:T(4,128)} %get-tuple-element.21), channel_id=1, source_target_pairs={{0,64},{64,128},{128,192},{192,256},{256,320},{320,384},{384,448},... | collective-permute-start | bytes 73736 | tf_op jit(solution)/shard_map/ppermute | solution.py:225
  21.2 2.0 %copy-start.1 = (f32[6,4,4,128]{3,2,1,0:T(4,128)}, f32[6,4,4,128]{3,2,1,0:T(4,128)S(1)}, u32[]{:S(2)}) copy-start(f32[6,4,4,128]{3,2,1,0:T(4,128)S(1)} %collective-permute-done.z_low) | copy-start | bytes 147460
  21.3 7.1 %collective-permute-start.5 = (f32[6,4,256]{2,1,0:T(4,128)}, f32[6,4,256]{2,1,0:T(4,128)S(1)}, u32[]{:S(2)}, u32[]{:S(2)}) collective-permute-start(f32[6,4,256]{2,1,0:T(4,128)} %get-tuple-element.22), channel_id=1, source_target_pairs={{0,448},{64,0},{128,64},{192,128},{256,192},{320,256},{384,320},{4... | collective-permute-start | bytes 73736 | tf_op jit(solution)/shard_map/ppermute | solution.py:225
  23.2 0.6 %copy-start.2 = (f32[6,4,4,128]{3,2,1,0:T(4,128)}, f32[6,4,4,128]{3,2,1,0:T(4,128)S(1)}, u32[]{:S(2)}) copy-start(f32[6,4,4,128]{3,2,1,0:T(4,128)S(1)} %collective-permute-done.1.z_high) | copy-start | bytes 147460
  23.2 0.6 %copy-start.3 = (f32[6,4,4,128]{3,2,1,0:T(4,128)}, f32[6,4,4,128]{3,2,1,0:T(4,128)S(1)}, u32[]{:S(2)}) copy-start(f32[6,4,4,128]{3,2,1,0:T(4,128)S(1)} %collective-permute-done.2.y_low) | copy-start | bytes 147460
  23.2 0.6 %copy-start.4 = (f32[6,4,4,128]{3,2,1,0:T(4,128)}, f32[6,4,4,128]{3,2,1,0:T(4,128)S(1)}, u32[]{:S(2)}) copy-start(f32[6,4,4,128]{3,2,1,0:T(4,128)S(1)} %collective-permute-done.3.y_high) | copy-start | bytes 147460
  27.0 1.4 %copy-start.5 = (f32[6,4,256]{2,1,0:T(4,128)}, f32[6,4,256]{2,1,0:T(4,128)S(1)}, u32[]{:S(2)}) copy-start(f32[6,4,256]{2,1,0:T(4,128)S(1)} %collective-permute-done.4.x_low) | copy-start | bytes 73732
  28.4 0.6 %copy-start.6 = (f32[6,4,256]{2,1,0:T(4,128)}, f32[6,4,256]{2,1,0:T(4,128)S(1)}, u32[]{:S(2)}) copy-start(f32[6,4,256]{2,1,0:T(4,128)S(1)} %collective-permute-done.5.x_high) | copy-start | bytes 73732
  31.3 3.5 %collective-permute-start.6 = (f32[2,6,16,256]{3,2,1,0:T(8,128)}, f32[2,6,16,256]{3,2,1,0:T(8,128)S(1)}, u32[]{:S(2)}, u32[]{:S(2)}) collective-permute-start(f32[2,6,16,256]{3,2,1,0:T(8,128)} %finish.1.own_ref), channel_id=1, source_target_pairs={{0,1},{1,0},{2,3},{3,2},{4,5},{5,4},{6,7},{7,6},{8,9},{9,8},{10,11... | collective-permute-start | bytes 589832 | tf_op jit(solution)/shard_map/ppermute | solution.py:242
  34.9 0.7 %copy-start = (f32[2,6,16,256]{3,2,1,0:T(8,128)}, f32[2,6,16,256]{3,2,1,0:T(8,128)S(1)}, u32[]{:S(2)}) copy-start(f32[2,6,16,256]{3,2,1,0:T(8,128)S(1)} %collective-permute-done.6.partner_ref) | copy-start | bytes 589828

commit v3 on v2

--- a/solution.py
+++ b/solution.py
@@ -16,6 +16,7 @@
 STEP_RATIO = 0.08
 VMEM = pl.BlockSpec(memory_space=pltpu.VMEM)
 ANY = pl.BlockSpec(memory_space=pl.ANY)
+PARAMS = pltpu.CompilerParams(vmem_limit_bytes=6 * 1024 * 1024)
 SMEM = pl.BlockSpec(memory_space=pltpu.SMEM)
 
 
@@ -144,7 +145,7 @@
             change[q, group] = value[GHOST : GHOST + EDGE]
 
 
-def lines_kernel(lines_z, lines_y, z_low, z_high, y_low, y_high, out_ref, change_z, change_y):
+def sides_kernel(prim_ref, lines_y, x_low, x_high, y_low, y_high, out_ref, change_y):
     slots = out_ref.shape[0]
     sweep_lines(y_low, lines_y, y_high, 1, change_y)
     for pair in range(0, FIELDS, 2):
@@ -153,15 +154,6 @@
             out_ref[:, pair + k] = parts[k].reshape(slots, EDGE, PLANE)
     flat = out_ref[...].reshape(slots * FIELDS * EDGE, PLANE)
     out_ref[...] = exchange_lanes(flat).reshape(slots, FIELDS, EDGE, PLANE)
-    sweep_lines(z_low, lines_z, z_high, 2, change_z)
-    for pair in range(0, FIELDS, 2):
-        parts = from_lines(change_z[pair].reshape(STRIP, HALF), change_z[pair + 1].reshape(STRIP, HALF))
-        for k in range(2):
-            out_ref[:, pair + k] += parts[k].reshape(slots, EDGE, PLANE)
-
-
-def finish_kernel(u_ref, prim_ref, change_ref, x_low, x_high, out_ref):
-    slots = u_ref.shape[0]
     for half in range(2):
         lanes = slice(half * HALF, half * HALF + HALF)
         lines = [
@@ -173,8 +165,17 @@
         for q, value in enumerate(sweep(lines, 0, row_at)):
             for p in range(slots):
                 first = GHOST + p * EDGE
-                total = change_ref[p, q, :, lanes] + value[first : first + EDGE]
-                out_ref[p, q, :, lanes] = u_ref[p, q, :, lanes] - STEP_RATIO * total
+                out_ref[p, q, :, lanes] += value[first : first + EDGE]
+
+
+def finish_kernel(u_ref, change_ref, lines_z, z_low, z_high, out_ref, change_z):
+    slots = u_ref.shape[0]
+    sweep_lines(z_low, lines_z, z_high, 2, change_z)
+    for pair in range(0, FIELDS, 2):
+        parts = from_lines(change_z[pair].reshape(STRIP, HALF), change_z[pair + 1].reshape(STRIP, HALF))
+        for k in range(2):
+            total = change_ref[:, pair + k] + parts[k].reshape(slots, EDGE, PLANE)
+            out_ref[:, pair + k] = u_ref[:, pair + k] - STEP_RATIO * total
 
 
 def place_kernel(index_ref, owner_ref, slot_ref, own_ref, partner_ref, out_ref, zeros, sems):
@@ -217,6 +218,7 @@
         out_shape=[block, lines, lines, x_side, x_side, side, side, side, side],
         in_specs=[VMEM],
         out_specs=[VMEM] * 9,
+        compiler_params=PARAMS,
         name="pack",
     )(patches)
 
@@ -224,20 +226,27 @@
         count = lax.axis_size(axis)
         return lax.ppermute(value, axis, [(i, (i + step) % count) for i in range(count)])
 
+    x_low, x_high = shift(x_up, "gx", 1), shift(x_down, "gx", -1)
+    y_low, y_high = shift(y_up, "gy", 1), shift(y_down, "gy", -1)
     z_low, z_high = shift(z_up, "gz", 1), shift(z_down, "gz", -1)
-    y_low, y_high = shift(y_up, "gy", 1), shift(y_down, "gy", -1)
-    x_low, x_high = shift(x_up, "gx", 1), shift(x_down, "gx", -1)
     change = pl.pallas_call(
-        lines_kernel,
+        sides_kernel,
         out_shape=block,
         in_specs=[VMEM] * 6,
         out_specs=VMEM,
-        scratch_shapes=[pltpu.VMEM(lines.shape, f32)] * 2,
-        name="lines",
-    )(lines_z, lines_y, z_low, z_high, y_low, y_high)
+        scratch_shapes=[pltpu.VMEM(lines.shape, f32)],
+        compiler_params=PARAMS,
+        name="sides",
+    )(prim, lines_y, x_low, x_high, y_low, y_high)
     advanced = pl.pallas_call(
-        finish_kernel, out_shape=block, in_specs=[VMEM] * 5, out_specs=VMEM, name="finish"
-    )(patches, prim, change, x_low, x_high)
+        finish_kernel,
+        out_shape=block,
+        in_specs=[VMEM] * 5,
+        out_specs=VMEM,
+        scratch_shapes=[pltpu.VMEM(lines.shape, f32)],
+        compiler_params=PARAMS,
+        name="finish",
+    )(patches, change, lines_z, z_low, z_high)
     members = lax.axis_size("gz")
     partner = lax.ppermute(advanced, "gz", [(i, i ^ 1) for i in range(members)])
     place = lax.axis_index("gz")
@@ -245,9 +254,10 @@
     return pl.pallas_call(
         place_kernel,
         out_shape=shape((CAP, FIELDS, EDGE, PLANE), f32),
-        in_specs=[SMEM, SMEM, SMEM, ANY, ANY],
+        in_specs=[SMEM, SMEM, SMEM, VMEM, VMEM],
         out_specs=ANY,
         scratch_shapes=[pltpu.VMEM((FIELDS, EDGE, PLANE), f32), pltpu.SemaphoreType.DMA((CAP,))],
+        compiler_params=PARAMS,
         name="place",
     )(jnp.stack([me, place]).astype(jnp.int32), new_owner, new_slot, advanced, partner)
 

time: 49.6 us -> 35.3 us (0.71)
  the two profiles are of different devices: /device:TPU:30 before, /device:TPU:25 now
where the time goes in v3:
time: 35.3 us; the launch traced here: 35 us
  starting transfers between devices  25.1 us (71%)
  waiting for transfers between devices  4.81 us (14%)
  Pallas kernels  4.04 us (11%)
  local copies, waits for them, and re-layouts  0.94 us (3%)
    ppermute x6, starting transfers between devices, shift(): lax.ppermute(value, axis, [(i, (i + step) % count) for i in range(count)])  16.3 us
    ppermute x1, starting transfers between devices, on_device(): partner = lax.ppermute(advanced, 'gz', [(i, i ^ 1) for i in range(members)])  8.74 us
    ppermute x6, waiting for transfers between devices, shift(): lax.ppermute(value, axis, [(i, (i + step) % count) for i in range(count)])  3.87 us
    pallas_call x1, Pallas kernels, on_device(): pl.pallas_call(place_kernel, out_shape=shape((CAP, FIELDS, EDGE, PLANE),...  1.35 us
    pallas_call x1, Pallas kernels, on_device(): pl.pallas_call(sides_kernel, out_shape=block, in_specs=[VMEM] * 6, out_sp...  1.33 us
    unnamed x8, local copies, waits for them, and re-layouts  0.94 us
    ppermute x1, waiting for transfers between devices, on_device(): partner = lax.ppermute(advanced, 'gz', [(i, i ^ 1) for i in range(members)])  0.94 us
    pallas_call x1, Pallas kernels, on_device(): pl.pallas_call(finish_kernel, out_shape=block, in_specs=[VMEM] * 5, out_s...  0.78 us
  transfers between devices with their start and end apart: 7, of which 2 were waited for; matrix products, arithmetic and copies ran while one was open for 0% of the time, Pallas kernels for 4%

profile of v3, /device:TPU:25, one launch (start us, length us, event | category | flops | bytes accessed | tf_op | source)
XLA Modules:
  0.0 35.0 jit_solution(15500967186446272554)
XLA Ops:
  0.0 0.9 %copy-done = f32[2,6,16,256]{3,2,1,0:T(8,128)S(1)} copy-done((f32[2,6,16,256]{3,2,1,0:T(8,128)S(1)}, f32[2,6,16,256]{3,2,1,0:T(8,128)}, u32[]{:S(2)}) %copy-start) | copy-done | bytes 196632
  0.9 0.6 %pack.1 = (f32[2,6,16,256]{3,2,1,0:T(8,128)S(1)}, f32[6,4,16,128]{3,2,1,0:T(8,128)S(1)}, f32[6,4,16,128]{3,2,1,0:T(8,128)S(1)}, f32[6,4,256]{2,1,0:T(4,128)S(1)}...) custom-call(f32[2,6,16,256]{3,2,1,0:T(8,128)S(1)} %copy-done), custom_call_target="tpu_custom_call" | custom-call | tf_op jit(solution)/shard_map/pack/pallas_call | solution.py:216
  1.5 4.4 %collective-permute-start = (f32[6,4,256]{2,1,0:T(4,128)S(1)}, f32[6,4,256]{2,1,0:T(4,128)S(1)}, u32[]{:S(2)}, u32[]{:S(2)}) collective-permute-start(f32[6,4,256]{2,1,0:T(4,128)S(1)} %get-tuple-element.16), channel_id=1, source_target_pairs={{0,64},{64,128},{128,192},{192,256},{256,320},{320,384},{384,448},... | collective-permute-start | bytes 73736 | tf_op jit(solution)/shard_map/ppermute | solution.py:227
  5.9 3.1 %collective-permute-start.2 = (f32[6,4,4,128]{3,2,1,0:T(4,128)S(1)}, f32[6,4,4,128]{3,2,1,0:T(4,128)S(1)}, u32[]{:S(2)}, u32[]{:S(2)}) collective-permute-start(f32[6,4,4,128]{3,2,1,0:T(4,128)S(1)} %get-tuple-element.18), channel_id=1, source_target_pairs={{0,16},{16,32},{32,48},{48,0},{1,17},{17,33},{33,49},{49,1},{2,18}... | collective-permute-start | bytes 147464 | tf_op jit(solution)/shard_map/ppermute | solution.py:227
  9.1 3.4 %collective-permute-start.3 = (f32[6,4,4,128]{3,2,1,0:T(4,128)S(1)}, f32[6,4,4,128]{3,2,1,0:T(4,128)S(1)}, u32[]{:S(2)}, u32[]{:S(2)}) collective-permute-start(f32[6,4,4,128]{3,2,1,0:T(4,128)S(1)} %get-tuple-element.19), channel_id=1, source_target_pairs={{0,48},{16,0},{32,16},{48,32},{1,49},{17,1},{33,17},{49,33},{2,50}... | collective-permute-start | bytes 147464 | tf_op jit(solution)/shard_map/ppermute | solution.py:227
  12.4 3.5 %collective-permute-start.4 = (f32[6,4,4,128]{3,2,1,0:T(4,128)S(1)}, f32[6,4,4,128]{3,2,1,0:T(4,128)S(1)}, u32[]{:S(2)}, u32[]{:S(2)}) collective-permute-start(f32[6,4,4,128]{3,2,1,0:T(4,128)S(1)} %get-tuple-element.21), channel_id=1, source_target_pairs={{0,1},{1,2},{2,3},{3,4},{4,5},{5,6},{6,7},{7,8},{8,9},{9,10},{10,1... | collective-permute-start | bytes 147464 | tf_op jit(solution)/shard_map/ppermute | solution.py:227
  15.9 0.0 collective-permute-start.5
  15.9 0.0 collective-permute-done.x_low
  16.0 1.9 %collective-permute-start.1 = (f32[6,4,256]{2,1,0:T(4,128)S(1)}, f32[6,4,256]{2,1,0:T(4,128)S(1)}, u32[]{:S(2)}, u32[]{:S(2)}) collective-permute-start(f32[6,4,256]{2,1,0:T(4,128)S(1)} %get-tuple-element.17), channel_id=1, source_target_pairs={{0,448},{64,0},{128,64},{192,128},{256,192},{320,256},{384,320},{4... | collective-permute-start | bytes 73736 | tf_op jit(solution)/shard_map/ppermute | solution.py:227
  17.9 3.9 %collective-permute-done.1.x_high = f32[6,4,256]{2,1,0:T(4,128)S(1)} collective-permute-done((f32[6,4,256]{2,1,0:T(4,128)S(1)}, f32[6,4,256]{2,1,0:T(4,128)S(1)}, u32[]{:S(2)}, u32[]{:S(2)}) %collective-permute-start.1) | collective-permute-done | bytes 24608 | tf_op jit(solution)/shard_map/ppermute | solution.py:227
  21.7 0.0 collective-permute-done.2.y_low
  21.7 0.0 collective-permute-done.3.y_high
  21.7 1.3 %sides.1.change_ref = f32[2,6,16,256]{3,2,1,0:T(8,128)S(1)} custom-call(f32[2,6,16,256]{3,2,1,0:T(8,128)S(1)} %get-tuple-element.14.prim_ref, f32[6,4,16,128]{3,2,1,0:T(8,128)S(1)} %get-tuple-element.15.lines_y, f32[6,4,256]{2,1,0:T(4,128)S(1)} %collective-permute-done.x_low, f32[6,4,256]{2,1,0:T(4,128)S(1)} %collective-permute-done.1.x_high, ...), custom_call_target="tpu_custom_call" | custom-call | tf_op jit(solution)/shard_map/sides/pallas_call | solution.py:232
  23.1 0.0 collective-permute-done.4.z_low
  23.1 0.0 collective-permute-done.5.z_high
  23.1 0.0 copy-done.1
  23.1 0.8 %finish.1.own_ref = f32[2,6,16,256]{3,2,1,0:T(8,128)S(1)} custom-call(f32[2,6,16,256]{3,2,1,0:T(8,128)S(1)} %copy-done.1, f32[2,6,16,256]{3,2,1,0:T(8,128)S(1)} %sides.1.change_ref, f32[6,4,16,128]{3,2,1,0:T(8,128)S(1)} %get-tuple-element.20.lines_z, f32[6,4,4,128]{3,2,1,0:T(4,128)S(1)} %collective-permute-done.4.z_low, ...), custom_call_target="tpu_custom_call" | custom-call | tf_op jit(solution)/shard_map/finish/pallas_call | solution.py:241
  23.9 8.7 %collective-permute-start.6 = (f32[2,6,16,256]{3,2,1,0:T(8,128)S(1)}, f32[2,6,16,256]{3,2,1,0:T(8,128)S(1)}, u32[]{:S(2)}, u32[]{:S(2)}) collective-permute-start(f32[2,6,16,256]{3,2,1,0:T(8,128)S(1)} %finish.1.own_ref), channel_id=1, source_target_pairs={{0,1},{1,0},{2,3},{3,2},{4,5},{5,4},{6,7},{7,6},{8,9},{9,8},{10,11... | collective-permute-start | bytes 589832 | tf_op jit(solution)/shard_map/ppermute | solution.py:251
  32.6 0.0 copy-start.2
  32.7 0.0 copy-start.3
  32.7 0.1 pad_add_fusion.index_ref
  32.7 0.9 %collective-permute-done.6.partner_ref = f32[2,6,16,256]{3,2,1,0:T(8,128)S(1)} collective-permute-done((f32[2,6,16,256]{3,2,1,0:T(8,128)S(1)}, f32[2,6,16,256]{3,2,1,0:T(8,128)S(1)}, u32[]{:S(2)}, u32[]{:S(2)}) %collective-permute-start.6) | collective-permute-done | bytes 196640 | tf_op jit(solution)/shard_map/ppermute | solution.py:251
  33.7 0.0 copy-done.3
  33.7 1.3 %place.1 = f32[4,6,16,256]{3,2,1,0:T(8,128)} custom-call(s32[2]{0:T(128)S(1)} %pad_add_fusion.index_ref, s32[32]{0:T(128)S(1)} %copy-done.2, s32[32]{0:T(128)S(1)} %copy-done.3, f32[2,6,16,256]{3,2,1,0:T(8,128)S(1)} %finish.1.own_ref, f32[2,6,16,256]{3,2,1,0:T(8,128)S(1)} %collective-permute-done.6.partner_ref), custom_call_target="tpu_custom_call" | custom-call | tf_op jit(solution)/shard_map/place/pallas_call | solution.py:254
  (3 shorter events, 0.0 us)
Async XLA Ops:
  0.0 0.9 %copy-start = (f32[2,6,16,256]{3,2,1,0:T(8,128)S(1)}, f32[2,6,16,256]{3,2,1,0:T(8,128)}, u32[]{:S(2)}) copy-start(f32[2,6,16,256]{3,2,1,0:T(8,128)} %u_ref.3) | copy-start | bytes 589828
  1.5 14.4 %collective-permute-start = (f32[6,4,256]{2,1,0:T(4,128)S(1)}, f32[6,4,256]{2,1,0:T(4,128)S(1)}, u32[]{:S(2)}, u32[]{:S(2)}) collective-permute-start(f32[6,4,256]{2,1,0:T(4,128)S(1)} %get-tuple-element.16), channel_id=1, source_target_pairs={{0,64},{64,128},{128,192},{192,256},{256,320},{320,384},{384,448},... | collective-permute-start | bytes 73736 | tf_op jit(solution)/shard_map/ppermute | solution.py:227
  5.9 15.8 %collective-permute-start.2 = (f32[6,4,4,128]{3,2,1,0:T(4,128)S(1)}, f32[6,4,4,128]{3,2,1,0:T(4,128)S(1)}, u32[]{:S(2)}, u32[]{:S(2)}) collective-permute-start(f32[6,4,4,128]{3,2,1,0:T(4,128)S(1)} %get-tuple-element.18), channel_id=1, source_target_pairs={{0,16},{16,32},{32,48},{48,0},{1,17},{17,33},{33,49},{49,1},{2,18}... | collective-permute-start | bytes 147464 | tf_op jit(solution)/shard_map/ppermute | solution.py:227
  9.1 12.7 %collective-permute-start.3 = (f32[6,4,4,128]{3,2,1,0:T(4,128)S(1)}, f32[6,4,4,128]{3,2,1,0:T(4,128)S(1)}, u32[]{:S(2)}, u32[]{:S(2)}) collective-permute-start(f32[6,4,4,128]{3,2,1,0:T(4,128)S(1)} %get-tuple-element.19), channel_id=1, source_target_pairs={{0,48},{16,0},{32,16},{48,32},{1,49},{17,1},{33,17},{49,33},{2,50}... | collective-permute-start | bytes 147464 | tf_op jit(solution)/shard_map/ppermute | solution.py:227
  12.4 10.6 %collective-permute-start.4 = (f32[6,4,4,128]{3,2,1,0:T(4,128)S(1)}, f32[6,4,4,128]{3,2,1,0:T(4,128)S(1)}, u32[]{:S(2)}, u32[]{:S(2)}) collective-permute-start(f32[6,4,4,128]{3,2,1,0:T(4,128)S(1)} %get-tuple-element.21), channel_id=1, source_target_pairs={{0,1},{1,2},{2,3},{3,4},{4,5},{5,6},{6,7},{7,8},{8,9},{9,10},{10,1... | collective-permute-start | bytes 147464 | tf_op jit(solution)/shard_map/ppermute | solution.py:227
  15.9 7.1 %collective-permute-start.5 = (f32[6,4,4,128]{3,2,1,0:T(4,128)S(1)}, f32[6,4,4,128]{3,2,1,0:T(4,128)S(1)}, u32[]{:S(2)}, u32[]{:S(2)}) collective-permute-start(f32[6,4,4,128]{3,2,1,0:T(4,128)S(1)} %get-tuple-element.22), channel_id=1, source_target_pairs={{0,15},{1,0},{2,1},{3,2},{4,3},{5,4},{6,5},{7,6},{8,7},{9,8},{10,9... | collective-permute-start | bytes 147464 | tf_op jit(solution)/shard_map/ppermute | solution.py:227
  16.0 5.8 %collective-permute-start.1 = (f32[6,4,256]{2,1,0:T(4,128)S(1)}, f32[6,4,256]{2,1,0:T(4,128)S(1)}, u32[]{:S(2)}, u32[]{:S(2)}) collective-permute-start(f32[6,4,256]{2,1,0:T(4,128)S(1)} %get-tuple-element.17), channel_id=1, source_target_pairs={{0,448},{64,0},{128,64},{192,128},{256,192},{320,256},{384,320},{4... | collective-permute-start | bytes 73736 | tf_op jit(solution)/shard_map/ppermute | solution.py:227
  21.7 1.4 %copy-start.1 = (f32[2,6,16,256]{3,2,1,0:T(8,128)S(1)}, f32[2,6,16,256]{3,2,1,0:T(8,128)}, u32[]{:S(2)}) copy-start(f32[2,6,16,256]{3,2,1,0:T(8,128)} %u_ref.3) | copy-start | bytes 589828
  23.9 9.8 %collective-permute-start.6 = (f32[2,6,16,256]{3,2,1,0:T(8,128)S(1)}, f32[2,6,16,256]{3,2,1,0:T(8,128)S(1)}, u32[]{:S(2)}, u32[]{:S(2)}) collective-permute-start(f32[2,6,16,256]{3,2,1,0:T(8,128)S(1)} %finish.1.own_ref), channel_id=1, source_target_pairs={{0,1},{1,0},{2,3},{3,2},{4,5},{5,4},{6,7},{7,6},{8,9},{9,8},{10,11... | collective-permute-start | bytes 589832 | tf_op jit(solution)/shard_map/ppermute | solution.py:251
  32.6 1.0 %copy-start.2 = (s32[32]{0:T(128)S(1)}, s32[32]{0:T(128)}, u32[]{:S(2)}) copy-start(s32[32]{0:T(128)} %owner_ref.1) | copy-start | bytes 388
  32.7 1.0 %copy-start.3 = (s32[32]{0:T(128)S(1)}, s32[32]{0:T(128)}, u32[]{:S(2)}) copy-start(s32[32]{0:T(128)} %slot_ref.1) | copy-start | bytes 388

commit v4 on v3

--- a/solution.py
+++ b/solution.py
@@ -178,31 +178,30 @@
             out_ref[:, pair + k] = u_ref[:, pair + k] - STEP_RATIO * total
 
 
-def place_kernel(index_ref, owner_ref, slot_ref, own_ref, partner_ref, out_ref, zeros, sems):
+def place_kernel(code_ref, own_ref, partner_ref, out_ref, zeros, sems):
     slots = own_ref.shape[0]
-    me, group_place = index_ref[0], index_ref[1]
-    first = (group_place // 2) * (2 * slots)
-    side = group_place % 2
     zeros[...] = jnp.zeros_like(zeros)
+    sources = [zeros] + [own_ref.at[p] for p in range(slots)] + [partner_ref.at[p] for p in range(slots)]
     for s in range(CAP):
-        empty = True
-        for member in range(2):
-            for p in range(slots):
-                k = first + member * slots + p
-                here = jnp.logical_and(owner_ref[k] == me, slot_ref[k] == s)
-                empty = jnp.logical_and(empty, jnp.logical_not(here))
-                for ref, wanted in ((own_ref, side == member), (partner_ref, side != member)):
-
-                    @pl.when(jnp.logical_and(here, wanted))
-                    def _(ref=ref, p=p, s=s):
-                        pltpu.make_async_copy(ref.at[p], out_ref.at[s], sems.at[s]).start()
-
-        @pl.when(empty)
-        def _(s=s):
-            pltpu.make_async_copy(zeros, out_ref.at[s], sems.at[s]).start()
+        for c, source in enumerate(sources):
+
+            @pl.when(code_ref[s] == c)
+            def _(source=source, s=s):
+                pltpu.make_async_copy(source, out_ref.at[s], sems.at[s]).start()
 
     for s in range(CAP):
         pltpu.make_async_copy(zeros, out_ref.at[s], sems.at[s]).wait()
+
+
+def slot_codes(new_owner, new_slot, slots):
+    members = lax.axis_size("gz")
+    place = lax.axis_index("gz")
+    me = (lax.axis_index("gx") * lax.axis_size("gy") + lax.axis_index("gy")) * members + place
+    patch = lax.broadcasted_iota(jnp.int32, (CAP, members * slots), 1)
+    slot = lax.broadcasted_iota(jnp.int32, (CAP, members * slots), 0)
+    code = patch % slots + 1 + jnp.where(patch // slots == place, 0, slots)
+    here = jnp.logical_and(new_owner[None, :] == me, new_slot[None, :] == slot)
+    return jnp.sum(jnp.where(here, code, 0), axis=1)
 
 
 def on_device(patches, new_owner, new_slot):
@@ -226,9 +225,13 @@
         count = lax.axis_size(axis)
         return lax.ppermute(value, axis, [(i, (i + step) % count) for i in range(count)])
 
-    x_low, x_high = shift(x_up, "gx", 1), shift(x_down, "gx", -1)
-    y_low, y_high = shift(y_up, "gy", 1), shift(y_down, "gy", -1)
-    z_low, z_high = shift(z_up, "gz", 1), shift(z_down, "gz", -1)
+    y_low = shift(y_up, "gy", 1)
+    y_high = shift(y_down, "gy", -1)
+    x_low = shift(x_up, "gx", 1)
+    x_high = shift(x_down, "gx", -1)
+    z_up, z_down, y_high = lax.optimization_barrier((z_up, z_down, y_high))
+    z_low = shift(z_up, "gz", 1)
+    z_high = shift(z_down, "gz", -1)
     change = pl.pallas_call(
         sides_kernel,
         out_shape=block,
@@ -247,19 +250,18 @@
         compiler_params=PARAMS,
         name="finish",
     )(patches, change, lines_z, z_low, z_high)
+    advanced, new_owner, new_slot = lax.optimization_barrier((advanced, new_owner, new_slot))
     members = lax.axis_size("gz")
     partner = lax.ppermute(advanced, "gz", [(i, i ^ 1) for i in range(members)])
-    place = lax.axis_index("gz")
-    me = (lax.axis_index("gx") * lax.axis_size("gy") + lax.axis_index("gy")) * members + place
     return pl.pallas_call(
         place_kernel,
         out_shape=shape((CAP, FIELDS, EDGE, PLANE), f32),
-        in_specs=[SMEM, SMEM, SMEM, VMEM, VMEM],
+        in_specs=[SMEM, VMEM, VMEM],
         out_specs=ANY,
         scratch_shapes=[pltpu.VMEM((FIELDS, EDGE, PLANE), f32), pltpu.SemaphoreType.DMA((CAP,))],
         compiler_params=PARAMS,
         name="place",
-    )(jnp.stack([me, place]).astype(jnp.int32), new_owner, new_slot, advanced, partner)
+    )(slot_codes(new_owner, new_slot, slots), advanced, partner)
 
 
 def solution(mesh):

time: 35.3 us -> 32 us (0.907)
  the two profiles are of different devices: /device:TPU:25 before, /device:TPU:1 now
where the time goes in v4:
time: 32 us; the launch traced here: 31.7 us
  starting transfers between devices  25.6 us (80%)
  Pallas kernels  4.01 us (13%)
  local copies, waits for them, and re-layouts  1.59 us (5%)
    ppermute x6, starting transfers between devices, shift(): lax.ppermute(value, axis, [(i, (i + step) % count) for i in range(count)])  19.8 us
    ppermute x1, starting transfers between devices, on_device(): partner = lax.ppermute(advanced, 'gz', [(i, i ^ 1) for i in range(members)])  5.79 us
    unnamed x8, local copies, waits for them, and re-layouts  1.59 us
    pallas_call x1, Pallas kernels, on_device(): pl.pallas_call(sides_kernel, out_shape=block, in_specs=[VMEM] * 6, out_sp...  1.33 us
    pallas_call x1, Pallas kernels, on_device(): pl.pallas_call(place_kernel, out_shape=shape((CAP, FIELDS, EDGE, PLANE),...  1.32 us
    pallas_call x1, Pallas kernels, on_device(): pl.pallas_call(finish_kernel, out_shape=block, in_specs=[VMEM] * 5, out_s...  0.78 us
  transfers between devices with their start and end apart: 7, of which 1 were waited for; matrix products, arithmetic and copies ran while one was open for 0% of the time, Pallas kernels for 4%

profile of v4, /device:TPU:1, one launch (start us, length us, event | category | flops | bytes accessed | tf_op | source)
XLA Modules:
  0.0 31.7 jit_solution(6772374324895871598)
XLA Ops:
  0.0 0.9 %copy-done = f32[2,6,16,256]{3,2,1,0:T(8,128)S(1)} copy-done((f32[2,6,16,256]{3,2,1,0:T(8,128)S(1)}, f32[2,6,16,256]{3,2,1,0:T(8,128)}, u32[]{:S(2)}) %copy-start) | copy-done | bytes 196632
  0.9 0.6 %pack.1 = (f32[2,6,16,256]{3,2,1,0:T(8,128)S(1)}, f32[6,4,16,128]{3,2,1,0:T(8,128)S(1)}, f32[6,4,16,128]{3,2,1,0:T(8,128)S(1)}, f32[6,4,256]{2,1,0:T(4,128)S(1)}...) custom-call(f32[2,6,16,256]{3,2,1,0:T(8,128)S(1)} %copy-done), custom_call_target="tpu_custom_call" | custom-call | tf_op jit(solution)/shard_map/pack/pallas_call | solution.py:215
  1.5 5.2 %collective-permute-start.3 = (f32[6,4,4,128]{3,2,1,0:T(4,128)S(1)}, f32[6,4,4,128]{3,2,1,0:T(4,128)S(1)}, u32[]{:S(2)}, u32[]{:S(2)}) collective-permute-start(f32[6,4,4,128]{3,2,1,0:T(4,128)S(1)} %get-tuple-element.27), channel_id=1, source_target_pairs={{0,48},{16,0},{32,16},{48,32},{1,49},{17,1},{33,17},{49,33},{2,50}... | collective-permute-start | bytes 147464 | tf_op jit(solution)/shard_map/ppermute | solution.py:226
  6.7 1.9 %collective-permute-start.2 = (f32[6,4,4,128]{3,2,1,0:T(4,128)S(1)}, f32[6,4,4,128]{3,2,1,0:T(4,128)S(1)}, u32[]{:S(2)}, u32[]{:S(2)}) collective-permute-start(f32[6,4,4,128]{3,2,1,0:T(4,128)S(1)} %get-tuple-element.24), channel_id=1, source_target_pairs={{0,16},{16,32},{32,48},{48,0},{1,17},{17,33},{33,49},{49,1},{2,18}... | collective-permute-start | bytes 147464 | tf_op jit(solution)/shard_map/ppermute | solution.py:226
  8.7 3.2 %collective-permute-start = (f32[6,4,256]{2,1,0:T(4,128)S(1)}, f32[6,4,256]{2,1,0:T(4,128)S(1)}, u32[]{:S(2)}, u32[]{:S(2)}) collective-permute-start(f32[6,4,256]{2,1,0:T(4,128)S(1)} %get-tuple-element.22), channel_id=1, source_target_pairs={{0,64},{64,128},{128,192},{192,256},{256,320},{320,384},{384,448},... | collective-permute-start | bytes 73736 | tf_op jit(solution)/shard_map/ppermute | solution.py:226
  11.9 3.8 %collective-permute-start.1 = (f32[6,4,256]{2,1,0:T(4,128)S(1)}, f32[6,4,256]{2,1,0:T(4,128)S(1)}, u32[]{:S(2)}, u32[]{:S(2)}) collective-permute-start(f32[6,4,256]{2,1,0:T(4,128)S(1)} %get-tuple-element.23), channel_id=1, source_target_pairs={{0,448},{64,0},{128,64},{192,128},{256,192},{320,256},{384,320},{4... | collective-permute-start | bytes 73736 | tf_op jit(solution)/shard_map/ppermute | solution.py:226
  15.7 0.0 collective-permute-done.3.y_high
  15.7 3.2 %collective-permute-start.4 = (f32[6,4,4,128]{3,2,1,0:T(4,128)S(1)}, f32[6,4,4,128]{3,2,1,0:T(4,128)S(1)}, u32[]{:S(2)}, u32[]{:S(2)}) collective-permute-start(f32[6,4,4,128]{3,2,1,0:T(4,128)S(1)} %get-tuple-element.30), channel_id=1, source_target_pairs={{0,1},{1,2},{2,3},{3,4},{4,5},{5,6},{6,7},{7,8},{8,9},{9,10},{10,1... | collective-permute-start | bytes 147464 | tf_op jit(solution)/shard_map/ppermute | solution.py:226
  19.0 2.4 %collective-permute-start.5 = (f32[6,4,4,128]{3,2,1,0:T(4,128)S(1)}, f32[6,4,4,128]{3,2,1,0:T(4,128)S(1)}, u32[]{:S(2)}, u32[]{:S(2)}) collective-permute-start(f32[6,4,4,128]{3,2,1,0:T(4,128)S(1)} %get-tuple-element.31), channel_id=1, source_target_pairs={{0,15},{1,0},{2,1},{3,2},{4,3},{5,4},{6,5},{7,6},{8,7},{9,8},{10,9... | collective-permute-start | bytes 147464 | tf_op jit(solution)/shard_map/ppermute | solution.py:226
  21.4 0.0 collective-permute-done.x_low
  21.4 0.0 collective-permute-done.1.x_high
  21.4 0.0 collective-permute-done.2.y_low
  21.4 0.0 copy-start.1
  21.4 1.3 %sides.1.change_ref = f32[2,6,16,256]{3,2,1,0:T(8,128)S(1)} custom-call(f32[2,6,16,256]{3,2,1,0:T(8,128)S(1)} %get-tuple-element.20.prim_ref, f32[6,4,16,128]{3,2,1,0:T(8,128)S(1)} %get-tuple-element.21.lines_y, f32[6,4,256]{2,1,0:T(4,128)S(1)} %collective-permute-done.x_low, f32[6,4,256]{2,1,0:T(4,128)S(1)} %collective-permute-done.1.x_high, ...), custom_call_target="tpu_custom_call" | custom-call | tf_op jit(solution)/shard_map/sides/pallas_call | solution.py:235
  22.8 0.0 collective-permute-done.4.z_low
  22.8 0.0 collective-permute-done.5.z_high
  22.8 0.0 copy-start.3
  22.8 0.8 %finish.1.own_ref = f32[2,6,16,256]{3,2,1,0:T(8,128)S(1)} custom-call(f32[2,6,16,256]{3,2,1,0:T(8,128)S(1)} %copy-done.1, f32[2,6,16,256]{3,2,1,0:T(8,128)S(1)} %sides.1.change_ref, f32[6,4,16,128]{3,2,1,0:T(8,128)S(1)} %get-tuple-element.29.lines_z, f32[6,4,4,128]{3,2,1,0:T(4,128)S(1)} %collective-permute-done.4.z_low, ...), custom_call_target="tpu_custom_call" | custom-call | tf_op jit(solution)/shard_map/finish/pallas_call | solution.py:244
  23.6 5.8 %collective-permute-start.6 = (f32[2,6,16,256]{3,2,1,0:T(8,128)S(1)}, f32[2,6,16,256]{3,2,1,0:T(8,128)S(1)}, u32[]{:S(2)}, u32[]{:S(2)}) collective-permute-start(f32[2,6,16,256]{3,2,1,0:T(8,128)S(1)} %finish.1.own_ref), channel_id=1, source_target_pairs={{0,1},{1,0},{2,3},{3,2},{4,5},{5,4},{6,7},{7,6},{8,9},{9,8},{10,11... | collective-permute-start | bytes 589832 | tf_op jit(solution)/shard_map/ppermute | solution.py:255
  29.4 0.0 copy-start.2
  29.4 0.6 %copy-done.2 = s32[32]{0:T(128)S(1)} copy-done((s32[32]{0:T(128)S(1)}, s32[32]{0:T(128)}, u32[]{:S(2)}) %copy-start.2) | copy-done | bytes 152
  30.1 0.1 select_reduce_fusion.code_ref
  30.2 0.2 collective-permute-done.6.partner_ref
  30.4 1.3 %place.1 = f32[4,6,16,256]{3,2,1,0:T(8,128)} custom-call(s32[4]{0:T(128)S(1)} %select_reduce_fusion.code_ref, f32[2,6,16,256]{3,2,1,0:T(8,128)S(1)} %finish.1.own_ref, f32[2,6,16,256]{3,2,1,0:T(8,128)S(1)} %collective-permute-done.6.partner_ref), custom_call_target="tpu_custom_call" | custom-call | tf_op jit(solution)/shard_map/place/pallas_call | solution.py:256
  (7 shorter events, 0.0 us)
Async XLA Ops:
  0.0 0.9 %copy-start = (f32[2,6,16,256]{3,2,1,0:T(8,128)S(1)}, f32[2,6,16,256]{3,2,1,0:T(8,128)}, u32[]{:S(2)}) copy-start(f32[2,6,16,256]{3,2,1,0:T(8,128)} %u_ref.3) | copy-start | bytes 589828
  1.5 14.2 %collective-permute-start.3 = (f32[6,4,4,128]{3,2,1,0:T(4,128)S(1)}, f32[6,4,4,128]{3,2,1,0:T(4,128)S(1)}, u32[]{:S(2)}, u32[]{:S(2)}) collective-permute-start(f32[6,4,4,128]{3,2,1,0:T(4,128)S(1)} %get-tuple-element.27), channel_id=1, source_target_pairs={{0,48},{16,0},{32,16},{48,32},{1,49},{17,1},{33,17},{49,33},{2,50}... | collective-permute-start | bytes 147464 | tf_op jit(solution)/shard_map/ppermute | solution.py:226
  6.7 14.7 %collective-permute-start.2 = (f32[6,4,4,128]{3,2,1,0:T(4,128)S(1)}, f32[6,4,4,128]{3,2,1,0:T(4,128)S(1)}, u32[]{:S(2)}, u32[]{:S(2)}) collective-permute-start(f32[6,4,4,128]{3,2,1,0:T(4,128)S(1)} %get-tuple-element.24), channel_id=1, source_target_pairs={{0,16},{16,32},{32,48},{48,0},{1,17},{17,33},{33,49},{49,1},{2,18}... | collective-permute-start | bytes 147464 | tf_op jit(solution)/shard_map/ppermute | solution.py:226
  8.7 12.7 %collective-permute-start = (f32[6,4,256]{2,1,0:T(4,128)S(1)}, f32[6,4,256]{2,1,0:T(4,128)S(1)}, u32[]{:S(2)}, u32[]{:S(2)}) collective-permute-start(f32[6,4,256]{2,1,0:T(4,128)S(1)} %get-tuple-element.22), channel_id=1, source_target_pairs={{0,64},{64,128},{128,192},{192,256},{256,320},{320,384},{384,448},... | collective-permute-start | bytes 73736 | tf_op jit(solution)/shard_map/ppermute | solution.py:226
  11.9 9.5 %collective-permute-start.1 = (f32[6,4,256]{2,1,0:T(4,128)S(1)}, f32[6,4,256]{2,1,0:T(4,128)S(1)}, u32[]{:S(2)}, u32[]{:S(2)}) collective-permute-start(f32[6,4,256]{2,1,0:T(4,128)S(1)} %get-tuple-element.23), channel_id=1, source_target_pairs={{0,448},{64,0},{128,64},{192,128},{256,192},{320,256},{384,320},{4... | collective-permute-start | bytes 73736 | tf_op jit(solution)/shard_map/ppermute | solution.py:226
  15.7 7.0 %collective-permute-start.4 = (f32[6,4,4,128]{3,2,1,0:T(4,128)S(1)}, f32[6,4,4,128]{3,2,1,0:T(4,128)S(1)}, u32[]{:S(2)}, u32[]{:S(2)}) collective-permute-start(f32[6,4,4,128]{3,2,1,0:T(4,128)S(1)} %get-tuple-element.30), channel_id=1, source_target_pairs={{0,1},{1,2},{2,3},{3,4},{4,5},{5,6},{6,7},{7,8},{8,9},{9,10},{10,1... | collective-permute-start | bytes 147464 | tf_op jit(solution)/shard_map/ppermute | solution.py:226
  19.0 3.8 %collective-permute-start.5 = (f32[6,4,4,128]{3,2,1,0:T(4,128)S(1)}, f32[6,4,4,128]{3,2,1,0:T(4,128)S(1)}, u32[]{:S(2)}, u32[]{:S(2)}) collective-permute-start(f32[6,4,4,128]{3,2,1,0:T(4,128)S(1)} %get-tuple-element.31), channel_id=1, source_target_pairs={{0,15},{1,0},{2,1},{3,2},{4,3},{5,4},{6,5},{7,6},{8,7},{9,8},{10,9... | collective-permute-start | bytes 147464 | tf_op jit(solution)/shard_map/ppermute | solution.py:226
  21.4 1.4 %copy-start.1 = (f32[2,6,16,256]{3,2,1,0:T(8,128)S(1)}, f32[2,6,16,256]{3,2,1,0:T(8,128)}, u32[]{:S(2)}) copy-start(f32[2,6,16,256]{3,2,1,0:T(8,128)} %u_ref.3) | copy-start | bytes 589828
  22.8 6.6 %copy-start.3 = (s32[32]{0:T(128)S(1)}, s32[32]{0:T(128)}, u32[]{:S(2)}) copy-start(s32[32]{0:T(128)} %param.4) | copy-start | bytes 388
  23.6 6.8 %collective-permute-start.6 = (f32[2,6,16,256]{3,2,1,0:T(8,128)S(1)}, f32[2,6,16,256]{3,2,1,0:T(8,128)S(1)}, u32[]{:S(2)}, u32[]{:S(2)}) collective-permute-start(f32[2,6,16,256]{3,2,1,0:T(8,128)S(1)} %finish.1.own_ref), channel_id=1, source_target_pairs={{0,1},{1,0},{2,3},{3,2},{4,5},{5,4},{6,7},{7,6},{8,9},{9,8},{10,11... | collective-permute-start | bytes 589832 | tf_op jit(solution)/shard_map/ppermute | solution.py:255
  29.4 0.7 %copy-start.2 = (s32[32]{0:T(128)S(1)}, s32[32]{0:T(128)}, u32[]{:S(2)}) copy-start(s32[32]{0:T(128)} %param.5) | copy-start | bytes 388

commit v5 on v4

--- a/solution.py
+++ b/solution.py
@@ -17,7 +17,6 @@
 VMEM = pl.BlockSpec(memory_space=pltpu.VMEM)
 ANY = pl.BlockSpec(memory_space=pl.ANY)
 PARAMS = pltpu.CompilerParams(vmem_limit_bytes=6 * 1024 * 1024)
-SMEM = pl.BlockSpec(memory_space=pltpu.SMEM)
 
 
 def to_primitive(u):
@@ -110,13 +109,11 @@
     return jnp.concatenate(one, axis=1), jnp.concatenate(two, axis=1)
 
 
-def pack_kernel(u_ref, prim_ref, lines_z, lines_y, x_up, x_down, y_up, y_down, z_up, z_down):
+def pack_kernel(u_ref, prim_ref, lines_z, lines_y, y_up, y_down, z_up, z_down):
     slots = u_ref.shape[0]
     for p in range(slots):
         for q, value in enumerate(to_primitive([u_ref[p, q] for q in range(FIELDS)])):
             prim_ref[p, q] = value
-    x_up[...] = prim_ref[slots - 1, :, EDGE - GHOST :, :]
-    x_down[...] = prim_ref[0, :, :GHOST, :]
     swapped = exchange_lanes(prim_ref[...].reshape(slots * FIELDS * EDGE, PLANE))
     swapped = swapped.reshape(slots, FIELDS, EDGE, PLANE)
     for pair in range(0, FIELDS, 2):
@@ -145,27 +142,31 @@
             change[q, group] = value[GHOST : GHOST + EDGE]
 
 
-def sides_kernel(prim_ref, lines_y, x_low, x_high, y_low, y_high, out_ref, change_y):
+def rows_kernel(prim_ref, low_ref, high_ref, out_ref):
+    slots = out_ref.shape[0]
+    for half in range(2):
+        lanes = slice(half * HALF, half * HALF + HALF)
+        low = to_primitive([low_ref[slots - 1, q, EDGE - GHOST :, lanes] for q in range(FIELDS)])
+        high = to_primitive([high_ref[0, q, :GHOST, lanes] for q in range(FIELDS)])
+        lines = [
+            jnp.concatenate([low[q]] + [prim_ref[p, q, :, lanes] for p in range(slots)] + [high[q]], axis=0)
+            for q in range(FIELDS)
+        ]
+        for q, value in enumerate(sweep(lines, 0, row_at)):
+            for p in range(slots):
+                first = GHOST + p * EDGE
+                out_ref[p, q, :, lanes] = value[first : first + EDGE]
+
+
+def columns_kernel(before_ref, lines_y, y_low, y_high, out_ref, change_y):
     slots = out_ref.shape[0]
     sweep_lines(y_low, lines_y, y_high, 1, change_y)
     for pair in range(0, FIELDS, 2):
         parts = from_lines(change_y[pair].reshape(STRIP, HALF), change_y[pair + 1].reshape(STRIP, HALF))
         for k in range(2):
             out_ref[:, pair + k] = parts[k].reshape(slots, EDGE, PLANE)
-    flat = out_ref[...].reshape(slots * FIELDS * EDGE, PLANE)
-    out_ref[...] = exchange_lanes(flat).reshape(slots, FIELDS, EDGE, PLANE)
-    for half in range(2):
-        lanes = slice(half * HALF, half * HALF + HALF)
-        lines = [
-            jnp.concatenate(
-                [x_low[q, :, lanes]] + [prim_ref[p, q, :, lanes] for p in range(slots)] + [x_high[q, :, lanes]], axis=0
-            )
-            for q in range(FIELDS)
-        ]
-        for q, value in enumerate(sweep(lines, 0, row_at)):
-            for p in range(slots):
-                first = GHOST + p * EDGE
-                out_ref[p, q, :, lanes] += value[first : first + EDGE]
+    flat = exchange_lanes(out_ref[...].reshape(slots * FIELDS * EDGE, PLANE))
+    out_ref[...] = flat.reshape(slots, FIELDS, EDGE, PLANE) + before_ref[...]
 
 
 def finish_kernel(u_ref, change_ref, lines_z, z_low, z_high, out_ref, change_z):
@@ -178,19 +179,23 @@
             out_ref[:, pair + k] = u_ref[:, pair + k] - STEP_RATIO * total
 
 
-def place_kernel(code_ref, own_ref, partner_ref, out_ref, zeros, sems):
+def place_kernel(code_ref, own_ref, partner_ref, out_ref, held, sems):
     slots = own_ref.shape[0]
-    zeros[...] = jnp.zeros_like(zeros)
-    sources = [zeros] + [own_ref.at[p] for p in range(slots)] + [partner_ref.at[p] for p in range(slots)]
+    copies = []
     for s in range(CAP):
-        for c, source in enumerate(sources):
-
-            @pl.when(code_ref[s] == c)
-            def _(source=source, s=s):
-                pltpu.make_async_copy(source, out_ref.at[s], sems.at[s]).start()
-
-    for s in range(CAP):
-        pltpu.make_async_copy(zeros, out_ref.at[s], sems.at[s]).wait()
+        code = jnp.concatenate([code_ref[s]] * 2, axis=1)
+        for q in range(FIELDS):
+            for half in range(2):
+                rows = slice(half * 8, half * 8 + 8)
+                value = jnp.zeros((8, PLANE), jnp.float32)
+                for p in range(slots):
+                    value = jnp.where(code == 1 + p, own_ref[p, q, rows, :], value)
+                    value = jnp.where(code == 1 + slots + p, partner_ref[p, q, rows, :], value)
+                held[s, q, rows, :] = value
+        copies.append(pltpu.make_async_copy(held.at[s], out_ref.at[s], sems.at[s]))
+        copies[s].start()
+    for copy in copies:
+        copy.wait()
 
 
 def slot_codes(new_owner, new_slot, slots):
@@ -201,7 +206,7 @@
     slot = lax.broadcasted_iota(jnp.int32, (CAP, members * slots), 0)
     code = patch % slots + 1 + jnp.where(patch // slots == place, 0, slots)
     here = jnp.logical_and(new_owner[None, :] == me, new_slot[None, :] == slot)
-    return jnp.sum(jnp.where(here, code, 0), axis=1)
+    return jnp.broadcast_to(jnp.sum(jnp.where(here, code, 0), axis=1)[:, None, None], (CAP, 8, HALF))
 
 
 def on_device(patches, new_owner, new_slot):
@@ -210,37 +215,36 @@
     shape = jax.ShapeDtypeStruct
     block = shape((slots, FIELDS, EDGE, PLANE), f32)
     lines = shape((FIELDS, GHOST, EDGE, HALF), f32)
-    x_side = shape((FIELDS, GHOST, PLANE), f32)
     side = shape((FIELDS, GHOST, GHOST, HALF), f32)
-    prim, lines_z, lines_y, x_up, x_down, y_up, y_down, z_up, z_down = pl.pallas_call(
-        pack_kernel,
-        out_shape=[block, lines, lines, x_side, x_side, side, side, side, side],
-        in_specs=[VMEM],
-        out_specs=[VMEM] * 9,
-        compiler_params=PARAMS,
-        name="pack",
-    )(patches)
 
     def shift(value, axis, step):
         count = lax.axis_size(axis)
         return lax.ppermute(value, axis, [(i, (i + step) % count) for i in range(count)])
 
-    y_low = shift(y_up, "gy", 1)
-    y_high = shift(y_down, "gy", -1)
-    x_low = shift(x_up, "gx", 1)
-    x_high = shift(x_down, "gx", -1)
+    x_low, x_high = shift(patches, "gx", 1), shift(patches, "gx", -1)
+    prim, lines_z, lines_y, y_up, y_down, z_up, z_down = pl.pallas_call(
+        pack_kernel,
+        out_shape=[block, lines, lines, side, side, side, side],
+        in_specs=[VMEM],
+        out_specs=[VMEM] * 7,
+        compiler_params=PARAMS,
+        name="pack",
+    )(patches)
+    y_low, y_high = shift(y_up, "gy", 1), shift(y_down, "gy", -1)
     z_up, z_down, y_high = lax.optimization_barrier((z_up, z_down, y_high))
-    z_low = shift(z_up, "gz", 1)
-    z_high = shift(z_down, "gz", -1)
+    z_low, z_high = shift(z_up, "gz", 1), shift(z_down, "gz", -1)
+    change_x = pl.pallas_call(
+        rows_kernel, out_shape=block, in_specs=[VMEM] * 3, out_specs=VMEM, compiler_params=PARAMS, name="rows"
+    )(prim, x_low, x_high)
     change = pl.pallas_call(
-        sides_kernel,
+        columns_kernel,
         out_shape=block,
-        in_specs=[VMEM] * 6,
+        in_specs=[VMEM] * 4,
         out_specs=VMEM,
         scratch_shapes=[pltpu.VMEM(lines.shape, f32)],
         compiler_params=PARAMS,
-        name="sides",
-    )(prim, lines_y, x_low, x_high, y_low, y_high)
+        name="columns",
+    )(change_x, lines_y, y_low, y_high)
     advanced = pl.pallas_call(
         finish_kernel,
         out_shape=block,
@@ -256,9 +260,9 @@
     return pl.pallas_call(
         place_kernel,
         out_shape=shape((CAP, FIELDS, EDGE, PLANE), f32),
-        in_specs=[SMEM, VMEM, VMEM],
+        in_specs=[VMEM] * 3,
         out_specs=ANY,
-        scratch_shapes=[pltpu.VMEM((FIELDS, EDGE, PLANE), f32), pltpu.SemaphoreType.DMA((CAP,))],
+        scratch_shapes=[pltpu.VMEM((CAP, FIELDS, EDGE, PLANE), f32), pltpu.SemaphoreType.DMA((CAP,))],
         compiler_params=PARAMS,
         name="place",
     )(slot_codes(new_owner, new_slot, slots), advanced, partner)

time: 32 us -> 31.5 us (0.984)
  Pallas kernels: 4.01 us -> 3.6 us
    pallas_call x1, Pallas kernels: 1.32 us -> 0.8 us  [on_device(): pl.pallas_call(place_kernel, out_shape=shape((CAP, FIELDS, EDGE, PLANE),...]
    pallas_call x2 -> x3, Pallas kernels: 1.91 us -> 2.02 us  [the longest x1 0.95 us: on_device(): pl.pallas_call(columns_kernel, out_shape=block, in_specs=[VMEM] * 4, out_...]
  transfers between devices with their start and end apart: 7 -> 7, of which waited for: 1 -> 1; matrix products, arithmetic and copies ran while one was open for 0% -> 0% of each run, Pallas kernels for 4% -> 6%
where the time goes in v5:
time: 31.5 us; the launch traced here: 31.3 us
  starting transfers between devices  25.5 us (81%)
  Pallas kernels  3.6 us (11%)
  local copies, waits for them, and re-layouts  1.66 us (5%)
    ppermute x6, starting transfers between devices, shift(): lax.ppermute(value, axis, [(i, (i + step) % count) for i in range(count)])  19.9 us
    ppermute x1, starting transfers between devices, on_device(): partner = lax.ppermute(advanced, 'gz', [(i, i ^ 1) for i in range(members)])  5.61 us
    unnamed x8, local copies, waits for them, and re-layouts  1.59 us
    pallas_call x1, Pallas kernels, on_device(): pl.pallas_call(columns_kernel, out_shape=block, in_specs=[VMEM] * 4, out_...  0.95 us
    pallas_call x1, Pallas kernels, on_device(): pl.pallas_call(place_kernel, out_shape=shape((CAP, FIELDS, EDGE, PLANE),...  0.8 us
    pallas_call x1, Pallas kernels, on_device(): pl.pallas_call(finish_kernel, out_shape=block, in_specs=[VMEM] * 5, out_s...  0.78 us
  transfers between devices with their start and end apart: 7, of which 1 were waited for; matrix products, arithmetic and copies ran while one was open for 0% of the time, Pallas kernels for 6%

profile of v5, /device:TPU:1, one launch (start us, length us, event | category | flops | bytes accessed | tf_op | source)
XLA Modules:
  0.0 31.3 jit_solution(14107283199173537726)
XLA Ops:
  0.0 4.0 %collective-permute-start = (f32[2,6,16,256]{3,2,1,0:T(8,128)}, f32[2,6,16,256]{3,2,1,0:T(8,128)S(1)}, u32[]{:S(2)}, u32[]{:S(2)}) collective-permute-start(f32[2,6,16,256]{3,2,1,0:T(8,128)} %u_ref.3), channel_id=1, source_target_pairs={{0,64},{64,128},{128,192},{192,256},{256,320},{320,384},{384,448},... | collective-permute-start | bytes 589832 | tf_op jit(solution)/shard_map/ppermute | solution.py:222
  4.0 3.8 %collective-permute-start.1 = (f32[2,6,16,256]{3,2,1,0:T(8,128)}, f32[2,6,16,256]{3,2,1,0:T(8,128)S(1)}, u32[]{:S(2)}, u32[]{:S(2)}) collective-permute-start(f32[2,6,16,256]{3,2,1,0:T(8,128)} %u_ref.3), channel_id=1, source_target_pairs={{0,448},{64,0},{128,64},{192,128},{256,192},{320,256},{384,320},{4... | collective-permute-start | bytes 589832 | tf_op jit(solution)/shard_map/ppermute | solution.py:222
  7.9 0.0 copy-start
  7.9 0.9 %copy-done = f32[2,6,16,256]{3,2,1,0:T(8,128)S(1)} copy-done((f32[2,6,16,256]{3,2,1,0:T(8,128)S(1)}, f32[2,6,16,256]{3,2,1,0:T(8,128)}, u32[]{:S(2)}) %copy-start) | copy-done | bytes 196632
  8.8 0.6 %pack.1 = (f32[2,6,16,256]{3,2,1,0:T(8,128)S(1)}, f32[6,4,16,128]{3,2,1,0:T(8,128)S(1)}, f32[6,4,16,128]{3,2,1,0:T(8,128)S(1)}, f32[6,4,4,128]{3,2,1,0:T(4,128)S...) custom-call(f32[2,6,16,256]{3,2,1,0:T(8,128)S(1)} %copy-done), custom_call_target="tpu_custom_call" | custom-call | tf_op jit(solution)/shard_map/pack/pallas_call | solution.py:225
  9.4 4.4 %collective-permute-start.3 = (f32[6,4,4,128]{3,2,1,0:T(4,128)S(1)}, f32[6,4,4,128]{3,2,1,0:T(4,128)S(1)}, u32[]{:S(2)}, u32[]{:S(2)}) collective-permute-start(f32[6,4,4,128]{3,2,1,0:T(4,128)S(1)} %get-tuple-element.23), channel_id=1, source_target_pairs={{0,48},{16,0},{32,16},{48,32},{1,49},{17,1},{33,17},{49,33},{2,50}... | collective-permute-start | bytes 147464 | tf_op jit(solution)/shard_map/ppermute | solution.py:222
  13.8 1.9 %collective-permute-start.2 = (f32[6,4,4,128]{3,2,1,0:T(4,128)S(1)}, f32[6,4,4,128]{3,2,1,0:T(4,128)S(1)}, u32[]{:S(2)}, u32[]{:S(2)}) collective-permute-start(f32[6,4,4,128]{3,2,1,0:T(4,128)S(1)} %get-tuple-element.20), channel_id=1, source_target_pairs={{0,16},{16,32},{32,48},{48,0},{1,17},{17,33},{33,49},{49,1},{2,18}... | collective-permute-start | bytes 147464 | tf_op jit(solution)/shard_map/ppermute | solution.py:222
  15.7 0.0 collective-permute-done.3.y_high
  15.7 3.2 %collective-permute-start.4 = (f32[6,4,4,128]{3,2,1,0:T(4,128)S(1)}, f32[6,4,4,128]{3,2,1,0:T(4,128)S(1)}, u32[]{:S(2)}, u32[]{:S(2)}) collective-permute-start(f32[6,4,4,128]{3,2,1,0:T(4,128)S(1)} %get-tuple-element.26), channel_id=1, source_target_pairs={{0,1},{1,2},{2,3},{3,4},{4,5},{5,6},{6,7},{7,8},{8,9},{9,10},{10,1... | collective-permute-start | bytes 147464 | tf_op jit(solution)/shard_map/ppermute | solution.py:222
  18.9 2.5 %collective-permute-start.5 = (f32[6,4,4,128]{3,2,1,0:T(4,128)S(1)}, f32[6,4,4,128]{3,2,1,0:T(4,128)S(1)}, u32[]{:S(2)}, u32[]{:S(2)}) collective-permute-start(f32[6,4,4,128]{3,2,1,0:T(4,128)S(1)} %get-tuple-element.27), channel_id=1, source_target_pairs={{0,15},{1,0},{2,1},{3,2},{4,3},{5,4},{6,5},{7,6},{8,7},{9,8},{10,9... | collective-permute-start | bytes 147464 | tf_op jit(solution)/shard_map/ppermute | solution.py:222
  21.4 0.0 collective-permute-done.low_ref
  21.4 0.5 %rows.1.before_ref = f32[2,6,16,256]{3,2,1,0:T(8,128)S(1)} custom-call(f32[2,6,16,256]{3,2,1,0:T(8,128)S(1)} %get-tuple-element.18.prim_ref, f32[2,6,16,256]{3,2,1,0:T(8,128)S(1)} %collective-permute-done.low_ref, f32[2,6,16,256]{3,2,1,0:T(8,128)S(1)} %collective-permute-done.1.high_ref), custom_call_target="tpu_custom_call" | custom-call | tf_op jit(solution)/shard_map/rows/pallas_call | solution.py:236
  22.0 0.0 collective-permute-done.2.y_low
  22.0 0.0 copy-start.1
  22.0 0.9 %columns.1.change_ref = f32[2,6,16,256]{3,2,1,0:T(8,128)S(1)} custom-call(f32[2,6,16,256]{3,2,1,0:T(8,128)S(1)} %rows.1.before_ref, f32[6,4,16,128]{3,2,1,0:T(8,128)S(1)} %get-tuple-element.19.lines_y, f32[6,4,4,128]{3,2,1,0:T(4,128)S(1)} %collective-permute-done.2.y_low, f32[6,4,4,128]{3,2,1,0:T(4,128)S(1)} %collective-permute-done.3.y_high), custom_call_target="tpu_custom_call" | custom-call | tf_op jit(solution)/shard_map/columns/pallas_call | solution.py:239
  23.0 0.0 copy-start.3
  23.0 0.8 %finish.1.own_ref = f32[2,6,16,256]{3,2,1,0:T(8,128)S(1)} custom-call(f32[2,6,16,256]{3,2,1,0:T(8,128)S(1)} %copy-done.1, f32[2,6,16,256]{3,2,1,0:T(8,128)S(1)} %columns.1.change_ref, f32[6,4,16,128]{3,2,1,0:T(8,128)S(1)} %get-tuple-element.25.lines_z, f32[6,4,4,128]{3,2,1,0:T(4,128)S(1)} %collective-permute-done.4.z_low, ...), custom_call_target="tpu_custom_call" | custom-call | tf_op jit(solution)/shard_map/finish/pallas_call | solution.py:248
  23.8 5.6 %collective-permute-start.6 = (f32[2,6,16,256]{3,2,1,0:T(8,128)S(1)}, f32[2,6,16,256]{3,2,1,0:T(8,128)S(1)}, u32[]{:S(2)}, u32[]{:S(2)}) collective-permute-start(f32[2,6,16,256]{3,2,1,0:T(8,128)S(1)} %finish.1.own_ref), channel_id=1, source_target_pairs={{0,1},{1,0},{2,3},{3,2},{4,5},{5,4},{6,7},{7,6},{8,9},{9,8},{10,11... | collective-permute-start | bytes 589832 | tf_op jit(solution)/shard_map/ppermute | solution.py:259
  29.4 0.0 copy-start.2
  29.4 0.6 %copy-done.2 = s32[32]{0:T(128)S(1)} copy-done((s32[32]{0:T(128)S(1)}, s32[32]{0:T(128)}, u32[]{:S(2)}) %copy-start.2) | copy-done | bytes 152
  30.1 0.1 select_reduce_fusion
  30.2 0.2 collective-permute-done.6.partner_ref
  30.4 0.1 broadcast_in_dim.8.code_ref
  30.5 0.8 %place.1 = f32[4,6,16,256]{3,2,1,0:T(8,128)} custom-call(s32[4,8,128]{2,1,0:T(8,128)S(1)} %broadcast_in_dim.8.code_ref, f32[2,6,16,256]{3,2,1,0:T(8,128)S(1)} %finish.1.own_ref, f32[2,6,16,256]{3,2,1,0:T(8,128)S(1)} %collective-permute-done.6.partner_ref), custom_call_target="tpu_custom_call" | custom-call | tf_op jit(solution)/shard_map/place/pallas_call | solution.py:260
  (9 shorter events, 0.0 us)
Async XLA Ops:
  0.0 21.4 %collective-permute-start = (f32[2,6,16,256]{3,2,1,0:T(8,128)}, f32[2,6,16,256]{3,2,1,0:T(8,128)S(1)}, u32[]{:S(2)}, u32[]{:S(2)}) collective-permute-start(f32[2,6,16,256]{3,2,1,0:T(8,128)} %u_ref.3), channel_id=1, source_target_pairs={{0,64},{64,128},{128,192},{192,256},{256,320},{320,384},{384,448},... | collective-permute-start | bytes 589832 | tf_op jit(solution)/shard_map/ppermute | solution.py:222
  4.0 17.4 %collective-permute-start.1 = (f32[2,6,16,256]{3,2,1,0:T(8,128)}, f32[2,6,16,256]{3,2,1,0:T(8,128)S(1)}, u32[]{:S(2)}, u32[]{:S(2)}) collective-permute-start(f32[2,6,16,256]{3,2,1,0:T(8,128)} %u_ref.3), channel_id=1, source_target_pairs={{0,448},{64,0},{128,64},{192,128},{256,192},{320,256},{384,320},{4... | collective-permute-start | bytes 589832 | tf_op jit(solution)/shard_map/ppermute | solution.py:222
  7.9 0.9 %copy-start = (f32[2,6,16,256]{3,2,1,0:T(8,128)S(1)}, f32[2,6,16,256]{3,2,1,0:T(8,128)}, u32[]{:S(2)}) copy-start(f32[2,6,16,256]{3,2,1,0:T(8,128)} %u_ref.3) | copy-start | bytes 589828
  9.4 6.3 %collective-permute-start.3 = (f32[6,4,4,128]{3,2,1,0:T(4,128)S(1)}, f32[6,4,4,128]{3,2,1,0:T(4,128)S(1)}, u32[]{:S(2)}, u32[]{:S(2)}) collective-permute-start(f32[6,4,4,128]{3,2,1,0:T(4,128)S(1)} %get-tuple-element.23), channel_id=1, source_target_pairs={{0,48},{16,0},{32,16},{48,32},{1,49},{17,1},{33,17},{49,33},{2,50}... | collective-permute-start | bytes 147464 | tf_op jit(solution)/shard_map/ppermute | solution.py:222
  13.8 8.2 %collective-permute-start.2 = (f32[6,4,4,128]{3,2,1,0:T(4,128)S(1)}, f32[6,4,4,128]{3,2,1,0:T(4,128)S(1)}, u32[]{:S(2)}, u32[]{:S(2)}) collective-permute-start(f32[6,4,4,128]{3,2,1,0:T(4,128)S(1)} %get-tuple-element.20), channel_id=1, source_target_pairs={{0,16},{16,32},{32,48},{48,0},{1,17},{17,33},{33,49},{49,1},{2,18}... | collective-permute-start | bytes 147464 | tf_op jit(solution)/shard_map/ppermute | solution.py:222
  15.7 7.2 %collective-permute-start.4 = (f32[6,4,4,128]{3,2,1,0:T(4,128)S(1)}, f32[6,4,4,128]{3,2,1,0:T(4,128)S(1)}, u32[]{:S(2)}, u32[]{:S(2)}) collective-permute-start(f32[6,4,4,128]{3,2,1,0:T(4,128)S(1)} %get-tuple-element.26), channel_id=1, source_target_pairs={{0,1},{1,2},{2,3},{3,4},{4,5},{5,6},{6,7},{7,8},{8,9},{9,10},{10,1... | collective-permute-start | bytes 147464 | tf_op jit(solution)/shard_map/ppermute | solution.py:222
  18.9 4.0 %collective-permute-start.5 = (f32[6,4,4,128]{3,2,1,0:T(4,128)S(1)}, f32[6,4,4,128]{3,2,1,0:T(4,128)S(1)}, u32[]{:S(2)}, u32[]{:S(2)}) collective-permute-start(f32[6,4,4,128]{3,2,1,0:T(4,128)S(1)} %get-tuple-element.27), channel_id=1, source_target_pairs={{0,15},{1,0},{2,1},{3,2},{4,3},{5,4},{6,5},{7,6},{8,7},{9,8},{10,9... | collective-permute-start | bytes 147464 | tf_op jit(solution)/shard_map/ppermute | solution.py:222
  22.0 1.0 %copy-start.1 = (f32[2,6,16,256]{3,2,1,0:T(8,128)S(1)}, f32[2,6,16,256]{3,2,1,0:T(8,128)}, u32[]{:S(2)}) copy-start(f32[2,6,16,256]{3,2,1,0:T(8,128)} %u_ref.3) | copy-start | bytes 589828
  23.0 6.4 %copy-start.3 = (s32[32]{0:T(128)S(1)}, s32[32]{0:T(128)}, u32[]{:S(2)}) copy-start(s32[32]{0:T(128)} %param.4) | copy-start | bytes 388
  23.8 6.7 %collective-permute-start.6 = (f32[2,6,16,256]{3,2,1,0:T(8,128)S(1)}, f32[2,6,16,256]{3,2,1,0:T(8,128)S(1)}, u32[]{:S(2)}, u32[]{:S(2)}) collective-permute-start(f32[2,6,16,256]{3,2,1,0:T(8,128)S(1)} %finish.1.own_ref), channel_id=1, source_target_pairs={{0,1},{1,0},{2,3},{3,2},{4,5},{5,4},{6,7},{7,6},{8,9},{9,8},{10,11... | collective-permute-start | bytes 589832 | tf_op jit(solution)/shard_map/ppermute | solution.py:259
  29.4 0.7 %copy-start.2 = (s32[32]{0:T(128)S(1)}, s32[32]{0:T(128)}, u32[]{:S(2)}) copy-start(s32[32]{0:T(128)} %param.5) | copy-start | bytes 388

commit v6 on v5

--- a/solution.py
+++ b/solution.py
@@ -74,15 +74,15 @@
 def exchange_lanes(rows):
     source = lax.broadcasted_iota(jnp.int32, (PLANE, PLANE), 0)
     target = lax.broadcasted_iota(jnp.int32, (PLANE, PLANE), 1)
-    wanted = (target % EDGE) * EDGE + target // EDGE
+    wanted = ((target & (EDGE - 1)) << 4) | (target >> 4)
     swap = jnp.where(source == wanted, 1.0, 0.0).astype(jnp.bfloat16)
-    total = None
+    parts = []
     for _ in range(3):
-        part = rows.astype(jnp.bfloat16)
-        moved = jnp.dot(part, swap, preferred_element_type=jnp.float32)
-        total = moved if total is None else total + moved
-        rows = rows - part.astype(jnp.float32)
-    return total
+        parts.append(rows.astype(jnp.bfloat16))
+        rows = rows - parts[-1].astype(jnp.float32)
+    moved = jnp.dot(jnp.concatenate(parts, axis=0), swap, preferred_element_type=jnp.float32)
+    count = rows.shape[0]
+    return moved[:count] + moved[count : 2 * count] + moved[2 * count :]
 
 
 def to_lines(first, second):
@@ -221,7 +221,7 @@
         count = lax.axis_size(axis)
         return lax.ppermute(value, axis, [(i, (i + step) % count) for i in range(count)])
 
-    x_low, x_high = shift(patches, "gx", 1), shift(patches, "gx", -1)
+    x_high, x_low = shift(patches, "gx", -1), shift(patches, "gx", 1)
     prim, lines_z, lines_y, y_up, y_down, z_up, z_down = pl.pallas_call(
         pack_kernel,
         out_shape=[block, lines, lines, side, side, side, side],

time: 31.5 us -> 31.5 us (level)
  no operation moved by 1% of the time
where the time goes in v6:
time: 31.5 us; the launch traced here: 31.3 us
  starting transfers between devices  25.5 us (81%)
  Pallas kernels  3.58 us (11%)
  local copies, waits for them, and re-layouts  1.66 us (5%)
    ppermute x6, starting transfers between devices, shift(): lax.ppermute(value, axis, [(i, (i + step) % count) for i in range(count)])  19.8 us
    ppermute x1, starting transfers between devices, on_device(): partner = lax.ppermute(advanced, 'gz', [(i, i ^ 1) for i in range(members)])  5.63 us
    unnamed x8, local copies, waits for them, and re-layouts  1.59 us
    pallas_call x1, Pallas kernels, on_device(): pl.pallas_call(columns_kernel, out_shape=block, in_specs=[VMEM] * 4, out_...  0.93 us
    pallas_call x1, Pallas kernels, on_device(): pl.pallas_call(place_kernel, out_shape=shape((CAP, FIELDS, EDGE, PLANE),...  0.8 us
    pallas_call x1, Pallas kernels, on_device(): pl.pallas_call(finish_kernel, out_shape=block, in_specs=[VMEM] * 5, out_s...  0.78 us
  transfers between devices with their start and end apart: 7, of which 1 were waited for; matrix products, arithmetic and copies ran while one was open for 0% of the time, Pallas kernels for 6%

profile of v6, /device:TPU:1, one launch (start us, length us, event | category | flops | bytes accessed | tf_op | source)
XLA Modules:
  0.0 31.3 jit_solution(14103942103683905694)
XLA Ops:
  0.0 4.0 %collective-permute-start = (f32[2,6,16,256]{3,2,1,0:T(8,128)}, f32[2,6,16,256]{3,2,1,0:T(8,128)S(1)}, u32[]{:S(2)}, u32[]{:S(2)}) collective-permute-start(f32[2,6,16,256]{3,2,1,0:T(8,128)} %u_ref.3), channel_id=1, source_target_pairs={{0,64},{64,128},{128,192},{192,256},{256,320},{320,384},{384,448},... | collective-permute-start | bytes 589832 | tf_op jit(solution)/shard_map/ppermute | solution.py:222
  4.0 3.8 %collective-permute-start.1 = (f32[2,6,16,256]{3,2,1,0:T(8,128)}, f32[2,6,16,256]{3,2,1,0:T(8,128)S(1)}, u32[]{:S(2)}, u32[]{:S(2)}) collective-permute-start(f32[2,6,16,256]{3,2,1,0:T(8,128)} %u_ref.3), channel_id=1, source_target_pairs={{0,448},{64,0},{128,64},{192,128},{256,192},{320,256},{384,320},{4... | collective-permute-start | bytes 589832 | tf_op jit(solution)/shard_map/ppermute | solution.py:222
  7.9 0.0 copy-start
  7.9 0.9 %copy-done = f32[2,6,16,256]{3,2,1,0:T(8,128)S(1)} copy-done((f32[2,6,16,256]{3,2,1,0:T(8,128)S(1)}, f32[2,6,16,256]{3,2,1,0:T(8,128)}, u32[]{:S(2)}) %copy-start) | copy-done | bytes 196632
  8.8 0.6 %pack.1 = (f32[2,6,16,256]{3,2,1,0:T(8,128)S(1)}, f32[6,4,16,128]{3,2,1,0:T(8,128)S(1)}, f32[6,4,16,128]{3,2,1,0:T(8,128)S(1)}, f32[6,4,4,128]{3,2,1,0:T(4,128)S...) custom-call(f32[2,6,16,256]{3,2,1,0:T(8,128)S(1)} %copy-done), custom_call_target="tpu_custom_call" | custom-call | tf_op jit(solution)/shard_map/pack/pallas_call | solution.py:225
  9.4 4.4 %collective-permute-start.3 = (f32[6,4,4,128]{3,2,1,0:T(4,128)S(1)}, f32[6,4,4,128]{3,2,1,0:T(4,128)S(1)}, u32[]{:S(2)}, u32[]{:S(2)}) collective-permute-start(f32[6,4,4,128]{3,2,1,0:T(4,128)S(1)} %get-tuple-element.23), channel_id=1, source_target_pairs={{0,48},{16,0},{32,16},{48,32},{1,49},{17,1},{33,17},{49,33},{2,50}... | collective-permute-start | bytes 147464 | tf_op jit(solution)/shard_map/ppermute | solution.py:222
  13.7 1.9 %collective-permute-start.2 = (f32[6,4,4,128]{3,2,1,0:T(4,128)S(1)}, f32[6,4,4,128]{3,2,1,0:T(4,128)S(1)}, u32[]{:S(2)}, u32[]{:S(2)}) collective-permute-start(f32[6,4,4,128]{3,2,1,0:T(4,128)S(1)} %get-tuple-element.20), channel_id=1, source_target_pairs={{0,16},{16,32},{32,48},{48,0},{1,17},{17,33},{33,49},{49,1},{2,18}... | collective-permute-start | bytes 147464 | tf_op jit(solution)/shard_map/ppermute | solution.py:222
  15.7 3.2 %collective-permute-start.4 = (f32[6,4,4,128]{3,2,1,0:T(4,128)S(1)}, f32[6,4,4,128]{3,2,1,0:T(4,128)S(1)}, u32[]{:S(2)}, u32[]{:S(2)}) collective-permute-start(f32[6,4,4,128]{3,2,1,0:T(4,128)S(1)} %get-tuple-element.26), channel_id=1, source_target_pairs={{0,1},{1,2},{2,3},{3,4},{4,5},{5,6},{6,7},{7,8},{8,9},{9,10},{10,1... | collective-permute-start | bytes 147464 | tf_op jit(solution)/shard_map/ppermute | solution.py:222
  18.9 2.5 %collective-permute-start.5 = (f32[6,4,4,128]{3,2,1,0:T(4,128)S(1)}, f32[6,4,4,128]{3,2,1,0:T(4,128)S(1)}, u32[]{:S(2)}, u32[]{:S(2)}) collective-permute-start(f32[6,4,4,128]{3,2,1,0:T(4,128)S(1)} %get-tuple-element.27), channel_id=1, source_target_pairs={{0,15},{1,0},{2,1},{3,2},{4,3},{5,4},{6,5},{7,6},{8,7},{9,8},{10,9... | collective-permute-start | bytes 147464 | tf_op jit(solution)/shard_map/ppermute | solution.py:222
  21.4 0.0 collective-permute-done.low_ref
  21.4 0.0 collective-permute-done.1.high_ref
  21.4 0.5 %rows.1.before_ref = f32[2,6,16,256]{3,2,1,0:T(8,128)S(1)} custom-call(f32[2,6,16,256]{3,2,1,0:T(8,128)S(1)} %get-tuple-element.18.prim_ref, f32[2,6,16,256]{3,2,1,0:T(8,128)S(1)} %collective-permute-done.low_ref, f32[2,6,16,256]{3,2,1,0:T(8,128)S(1)} %collective-permute-done.1.high_ref), custom_call_target="tpu_custom_call" | custom-call | tf_op jit(solution)/shard_map/rows/pallas_call | solution.py:236
  21.9 0.0 copy-start.1
  22.0 0.9 %columns.1.change_ref = f32[2,6,16,256]{3,2,1,0:T(8,128)S(1)} custom-call(f32[2,6,16,256]{3,2,1,0:T(8,128)S(1)} %rows.1.before_ref, f32[6,4,16,128]{3,2,1,0:T(8,128)S(1)} %get-tuple-element.19.lines_y, f32[6,4,4,128]{3,2,1,0:T(4,128)S(1)} %collective-permute-done.2.y_low, f32[6,4,4,128]{3,2,1,0:T(4,128)S(1)} %collective-permute-done.3.y_high), custom_call_target="tpu_custom_call" | custom-call | tf_op jit(solution)/shard_map/columns/pallas_call | solution.py:239
  22.9 0.0 collective-permute-done.4.z_low
  22.9 0.0 copy-start.3
  22.9 0.8 %finish.1.own_ref = f32[2,6,16,256]{3,2,1,0:T(8,128)S(1)} custom-call(f32[2,6,16,256]{3,2,1,0:T(8,128)S(1)} %copy-done.1, f32[2,6,16,256]{3,2,1,0:T(8,128)S(1)} %columns.1.change_ref, f32[6,4,16,128]{3,2,1,0:T(8,128)S(1)} %get-tuple-element.25.lines_z, f32[6,4,4,128]{3,2,1,0:T(4,128)S(1)} %collective-permute-done.4.z_low, ...), custom_call_target="tpu_custom_call" | custom-call | tf_op jit(solution)/shard_map/finish/pallas_call | solution.py:248
  23.7 5.6 %collective-permute-start.6 = (f32[2,6,16,256]{3,2,1,0:T(8,128)S(1)}, f32[2,6,16,256]{3,2,1,0:T(8,128)S(1)}, u32[]{:S(2)}, u32[]{:S(2)}) collective-permute-start(f32[2,6,16,256]{3,2,1,0:T(8,128)S(1)} %finish.1.own_ref), channel_id=1, source_target_pairs={{0,1},{1,0},{2,3},{3,2},{4,5},{5,4},{6,7},{7,6},{8,9},{9,8},{10,11... | collective-permute-start | bytes 589832 | tf_op jit(solution)/shard_map/ppermute | solution.py:259
  29.4 0.0 copy-start.2
  29.4 0.6 %copy-done.2 = s32[32]{0:T(128)S(1)} copy-done((s32[32]{0:T(128)S(1)}, s32[32]{0:T(128)}, u32[]{:S(2)}) %copy-start.2) | copy-done | bytes 152
  30.0 0.1 select_reduce_fusion
  30.2 0.2 collective-permute-done.6.partner_ref
  30.4 0.1 broadcast_in_dim.8.code_ref
  30.5 0.8 %place.1 = f32[4,6,16,256]{3,2,1,0:T(8,128)} custom-call(s32[4,8,128]{2,1,0:T(8,128)S(1)} %broadcast_in_dim.8.code_ref, f32[2,6,16,256]{3,2,1,0:T(8,128)S(1)} %finish.1.own_ref, f32[2,6,16,256]{3,2,1,0:T(8,128)S(1)} %collective-permute-done.6.partner_ref), custom_call_target="tpu_custom_call" | custom-call | tf_op jit(solution)/shard_map/place/pallas_call | solution.py:260
  (9 shorter events, 0.0 us)
Async XLA Ops:
  0.0 21.4 %collective-permute-start = (f32[2,6,16,256]{3,2,1,0:T(8,128)}, f32[2,6,16,256]{3,2,1,0:T(8,128)S(1)}, u32[]{:S(2)}, u32[]{:S(2)}) collective-permute-start(f32[2,6,16,256]{3,2,1,0:T(8,128)} %u_ref.3), channel_id=1, source_target_pairs={{0,64},{64,128},{128,192},{192,256},{256,320},{320,384},{384,448},... | collective-permute-start | bytes 589832 | tf_op jit(solution)/shard_map/ppermute | solution.py:222
  4.0 17.4 %collective-permute-start.1 = (f32[2,6,16,256]{3,2,1,0:T(8,128)}, f32[2,6,16,256]{3,2,1,0:T(8,128)S(1)}, u32[]{:S(2)}, u32[]{:S(2)}) collective-permute-start(f32[2,6,16,256]{3,2,1,0:T(8,128)} %u_ref.3), channel_id=1, source_target_pairs={{0,448},{64,0},{128,64},{192,128},{256,192},{320,256},{384,320},{4... | collective-permute-start | bytes 589832 | tf_op jit(solution)/shard_map/ppermute | solution.py:222
  7.9 0.9 %copy-start = (f32[2,6,16,256]{3,2,1,0:T(8,128)S(1)}, f32[2,6,16,256]{3,2,1,0:T(8,128)}, u32[]{:S(2)}) copy-start(f32[2,6,16,256]{3,2,1,0:T(8,128)} %u_ref.3) | copy-start | bytes 589828
  9.4 6.3 %collective-permute-start.3 = (f32[6,4,4,128]{3,2,1,0:T(4,128)S(1)}, f32[6,4,4,128]{3,2,1,0:T(4,128)S(1)}, u32[]{:S(2)}, u32[]{:S(2)}) collective-permute-start(f32[6,4,4,128]{3,2,1,0:T(4,128)S(1)} %get-tuple-element.23), channel_id=1, source_target_pairs={{0,48},{16,0},{32,16},{48,32},{1,49},{17,1},{33,17},{49,33},{2,50}... | collective-permute-start | bytes 147464 | tf_op jit(solution)/shard_map/ppermute | solution.py:222
  13.7 8.2 %collective-permute-start.2 = (f32[6,4,4,128]{3,2,1,0:T(4,128)S(1)}, f32[6,4,4,128]{3,2,1,0:T(4,128)S(1)}, u32[]{:S(2)}, u32[]{:S(2)}) collective-permute-start(f32[6,4,4,128]{3,2,1,0:T(4,128)S(1)} %get-tuple-element.20), channel_id=1, source_target_pairs={{0,16},{16,32},{32,48},{48,0},{1,17},{17,33},{33,49},{49,1},{2,18}... | collective-permute-start | bytes 147464 | tf_op jit(solution)/shard_map/ppermute | solution.py:222
  15.7 7.2 %collective-permute-start.4 = (f32[6,4,4,128]{3,2,1,0:T(4,128)S(1)}, f32[6,4,4,128]{3,2,1,0:T(4,128)S(1)}, u32[]{:S(2)}, u32[]{:S(2)}) collective-permute-start(f32[6,4,4,128]{3,2,1,0:T(4,128)S(1)} %get-tuple-element.26), channel_id=1, source_target_pairs={{0,1},{1,2},{2,3},{3,4},{4,5},{5,6},{6,7},{7,8},{8,9},{9,10},{10,1... | collective-permute-start | bytes 147464 | tf_op jit(solution)/shard_map/ppermute | solution.py:222
  18.9 4.0 %collective-permute-start.5 = (f32[6,4,4,128]{3,2,1,0:T(4,128)S(1)}, f32[6,4,4,128]{3,2,1,0:T(4,128)S(1)}, u32[]{:S(2)}, u32[]{:S(2)}) collective-permute-start(f32[6,4,4,128]{3,2,1,0:T(4,128)S(1)} %get-tuple-element.27), channel_id=1, source_target_pairs={{0,15},{1,0},{2,1},{3,2},{4,3},{5,4},{6,5},{7,6},{8,7},{9,8},{10,9... | collective-permute-start | bytes 147464 | tf_op jit(solution)/shard_map/ppermute | solution.py:222
  21.9 1.0 %copy-start.1 = (f32[2,6,16,256]{3,2,1,0:T(8,128)S(1)}, f32[2,6,16,256]{3,2,1,0:T(8,128)}, u32[]{:S(2)}) copy-start(f32[2,6,16,256]{3,2,1,0:T(8,128)} %u_ref.3) | copy-start | bytes 589828
  22.9 6.4 %copy-start.3 = (s32[32]{0:T(128)S(1)}, s32[32]{0:T(128)}, u32[]{:S(2)}) copy-start(s32[32]{0:T(128)} %param.4) | copy-start | bytes 388
  23.7 6.7 %collective-permute-start.6 = (f32[2,6,16,256]{3,2,1,0:T(8,128)S(1)}, f32[2,6,16,256]{3,2,1,0:T(8,128)S(1)}, u32[]{:S(2)}, u32[]{:S(2)}) collective-permute-start(f32[2,6,16,256]{3,2,1,0:T(8,128)S(1)} %finish.1.own_ref), channel_id=1, source_target_pairs={{0,1},{1,0},{2,3},{3,2},{4,5},{5,4},{6,7},{7,6},{8,9},{9,8},{10,11... | collective-permute-start | bytes 589832 | tf_op jit(solution)/shard_map/ppermute | solution.py:259
  29.4 0.7 %copy-start.2 = (s32[32]{0:T(128)S(1)}, s32[32]{0:T(128)}, u32[]{:S(2)}) copy-start(s32[32]{0:T(128)} %param.5) | copy-start | bytes 388

commit v7 on v6

--- a/solution.py
+++ b/solution.py
@@ -16,6 +16,7 @@
 STEP_RATIO = 0.08
 VMEM = pl.BlockSpec(memory_space=pltpu.VMEM)
 ANY = pl.BlockSpec(memory_space=pl.ANY)
+HELD = pltpu.VMEM((FIELDS, 2 * EDGE + 3 * 8, HALF), jnp.float32)
 PARAMS = pltpu.CompilerParams(vmem_limit_bytes=6 * 1024 * 1024)
 
 
@@ -42,11 +43,13 @@
     return speed, specific, signal
 
 
-def sweep(primitive, normal, at):
+def sweep(primitive, normal, at, held):
     plus, minus = [], []
-    for value in primitive:
-        after = at(value, 1)
-        face = 37.0 * (value + after) - 8.0 * (at(value, -1) + at(value, 2)) + (at(value, -2) + at(value, 3))
+    for q, value in enumerate(primitive):
+        count = value.shape[0]
+        held[q, 8 : 8 + count, :] = value
+        before2, before, after, after2, after3 = [held[q, 8 + k : 8 + k + count, :] for k in (-2, -1, 1, 2, 3)]
+        face = 37.0 * (value + after) - 8.0 * (before + after2) + (before2 + after3)
         face = face * (1.0 / 60.0)
         face = jnp.minimum(jnp.maximum(face, jnp.minimum(value, after)), jnp.maximum(value, after))
         left_jump = value - at(face, -1)
@@ -133,16 +136,16 @@
     return pltpu.roll(value, (-k) % height, 0)
 
 
-def sweep_lines(low, lines, high, normal, change):
+def sweep_lines(low, lines, high, normal, change, held):
     for group in range(GHOST):
         extended = [
             jnp.concatenate([low[q, group], lines[q, group], high[q, group]], axis=0) for q in range(FIELDS)
         ]
-        for q, value in enumerate(sweep(extended, normal, row_at)):
+        for q, value in enumerate(sweep(extended, normal, row_at, held)):
             change[q, group] = value[GHOST : GHOST + EDGE]
 
 
-def rows_kernel(prim_ref, low_ref, high_ref, out_ref):
+def rows_kernel(prim_ref, low_ref, high_ref, out_ref, held):
     slots = out_ref.shape[0]
     for half in range(2):
         lanes = slice(half * HALF, half * HALF + HALF)
@@ -152,15 +155,15 @@
             jnp.concatenate([low[q]] + [prim_ref[p, q, :, lanes] for p in range(slots)] + [high[q]], axis=0)
             for q in range(FIELDS)
         ]
-        for q, value in enumerate(sweep(lines, 0, row_at)):
+        for q, value in enumerate(sweep(lines, 0, row_at, held)):
             for p in range(slots):
                 first = GHOST + p * EDGE
                 out_ref[p, q, :, lanes] = value[first : first + EDGE]
 
 
-def columns_kernel(before_ref, lines_y, y_low, y_high, out_ref, change_y):
+def columns_kernel(before_ref, lines_y, y_low, y_high, out_ref, change_y, held):
     slots = out_ref.shape[0]
-    sweep_lines(y_low, lines_y, y_high, 1, change_y)
+    sweep_lines(y_low, lines_y, y_high, 1, change_y, held)
     for pair in range(0, FIELDS, 2):
         parts = from_lines(change_y[pair].reshape(STRIP, HALF), change_y[pair + 1].reshape(STRIP, HALF))
         for k in range(2):
@@ -169,9 +172,9 @@
     out_ref[...] = flat.reshape(slots, FIELDS, EDGE, PLANE) + before_ref[...]
 
 
-def finish_kernel(u_ref, change_ref, lines_z, z_low, z_high, out_ref, change_z):
+def finish_kernel(u_ref, change_ref, lines_z, z_low, z_high, out_ref, change_z, held):
     slots = u_ref.shape[0]
-    sweep_lines(z_low, lines_z, z_high, 2, change_z)
+    sweep_lines(z_low, lines_z, z_high, 2, change_z, held)
     for pair in range(0, FIELDS, 2):
         parts = from_lines(change_z[pair].reshape(STRIP, HALF), change_z[pair + 1].reshape(STRIP, HALF))
         for k in range(2):
@@ -234,14 +237,14 @@
     z_up, z_down, y_high = lax.optimization_barrier((z_up, z_down, y_high))
     z_low, z_high = shift(z_up, "gz", 1), shift(z_down, "gz", -1)
     change_x = pl.pallas_call(
-        rows_kernel, out_shape=block, in_specs=[VMEM] * 3, out_specs=VMEM, compiler_params=PARAMS, name="rows"
+        rows_kernel, out_shape=block, in_specs=[VMEM] * 3, out_specs=VMEM, scratch_shapes=[HELD], compiler_params=PARAMS, name="rows"
     )(prim, x_low, x_high)
     change = pl.pallas_call(
         columns_kernel,
         out_shape=block,
         in_specs=[VMEM] * 4,
         out_specs=VMEM,
-        scratch_shapes=[pltpu.VMEM(lines.shape, f32)],
+        scratch_shapes=[pltpu.VMEM(lines.shape, f32), HELD],
         compiler_params=PARAMS,
         name="columns",
     )(change_x, lines_y, y_low, y_high)
@@ -250,7 +253,7 @@
         out_shape=block,
         in_specs=[VMEM] * 5,
         out_specs=VMEM,
-        scratch_shapes=[pltpu.VMEM(lines.shape, f32)],
+        scratch_shapes=[pltpu.VMEM(lines.shape, f32), HELD],
         compiler_params=PARAMS,
         name="finish",
     )(patches, change, lines_z, z_low, z_high)

time: 31.5 us -> 31.5 us (level)
  no operation moved by 1% of the time
where the time goes in v7:
time: 31.5 us; the launch traced here: 31.2 us
  starting transfers between devices  25.6 us (81%)
  Pallas kernels  3.34 us (11%)
  local copies, waits for them, and re-layouts  1.69 us (5%)
    ppermute x6, starting transfers between devices, shift(): lax.ppermute(value, axis, [(i, (i + step) % count) for i in range(count)])  19.8 us
    ppermute x1, starting transfers between devices, on_device(): partner = lax.ppermute(advanced, 'gz', [(i, i ^ 1) for i in range(members)])  5.77 us
    unnamed x8, local copies, waits for them, and re-layouts  1.62 us
    pallas_call x1, Pallas kernels, on_device(): pl.pallas_call(columns_kernel, out_shape=block, in_specs=[VMEM] * 4, out_...  0.86 us
    pallas_call x1, Pallas kernels, on_device(): pl.pallas_call(place_kernel, out_shape=shape((CAP, FIELDS, EDGE, PLANE),...  0.8 us
    pallas_call x1, Pallas kernels, on_device(): pl.pallas_call(finish_kernel, out_shape=block, in_specs=[VMEM] * 5, out_s...  0.69 us
  transfers between devices with their start and end apart: 7, of which 1 were waited for; matrix products, arithmetic and copies ran while one was open for 0% of the time, Pallas kernels for 6%

profile of v7, /device:TPU:1, one launch (start us, length us, event | category | flops | bytes accessed | tf_op | source)
XLA Modules:
  0.0 31.2 jit_solution(7467734347738449060)
XLA Ops:
  0.0 4.0 %collective-permute-start = (f32[2,6,16,256]{3,2,1,0:T(8,128)}, f32[2,6,16,256]{3,2,1,0:T(8,128)S(1)}, u32[]{:S(2)}, u32[]{:S(2)}) collective-permute-start(f32[2,6,16,256]{3,2,1,0:T(8,128)} %u_ref.3), channel_id=1, source_target_pairs={{0,64},{64,128},{128,192},{192,256},{256,320},{320,384},{384,448},... | collective-permute-start | bytes 589832 | tf_op jit(solution)/shard_map/ppermute | solution.py:225
  4.0 3.8 %collective-permute-start.1 = (f32[2,6,16,256]{3,2,1,0:T(8,128)}, f32[2,6,16,256]{3,2,1,0:T(8,128)S(1)}, u32[]{:S(2)}, u32[]{:S(2)}) collective-permute-start(f32[2,6,16,256]{3,2,1,0:T(8,128)} %u_ref.3), channel_id=1, source_target_pairs={{0,448},{64,0},{128,64},{192,128},{256,192},{320,256},{384,320},{4... | collective-permute-start | bytes 589832 | tf_op jit(solution)/shard_map/ppermute | solution.py:225
  7.9 0.0 copy-start
  7.9 0.9 %copy-done = f32[2,6,16,256]{3,2,1,0:T(8,128)S(1)} copy-done((f32[2,6,16,256]{3,2,1,0:T(8,128)S(1)}, f32[2,6,16,256]{3,2,1,0:T(8,128)}, u32[]{:S(2)}) %copy-start) | copy-done | bytes 196632
  8.8 0.6 %pack.1 = (f32[2,6,16,256]{3,2,1,0:T(8,128)S(1)}, f32[6,4,16,128]{3,2,1,0:T(8,128)S(1)}, f32[6,4,16,128]{3,2,1,0:T(8,128)S(1)}, f32[6,4,4,128]{3,2,1,0:T(4,128)S...) custom-call(f32[2,6,16,256]{3,2,1,0:T(8,128)S(1)} %copy-done), custom_call_target="tpu_custom_call" | custom-call | tf_op jit(solution)/shard_map/pack/pallas_call | solution.py:228
  9.4 4.4 %collective-permute-start.3 = (f32[6,4,4,128]{3,2,1,0:T(4,128)S(1)}, f32[6,4,4,128]{3,2,1,0:T(4,128)S(1)}, u32[]{:S(2)}, u32[]{:S(2)}) collective-permute-start(f32[6,4,4,128]{3,2,1,0:T(4,128)S(1)} %get-tuple-element.23), channel_id=1, source_target_pairs={{0,48},{16,0},{32,16},{48,32},{1,49},{17,1},{33,17},{49,33},{2,50}... | collective-permute-start | bytes 147464 | tf_op jit(solution)/shard_map/ppermute | solution.py:225
  13.7 1.9 %collective-permute-start.2 = (f32[6,4,4,128]{3,2,1,0:T(4,128)S(1)}, f32[6,4,4,128]{3,2,1,0:T(4,128)S(1)}, u32[]{:S(2)}, u32[]{:S(2)}) collective-permute-start(f32[6,4,4,128]{3,2,1,0:T(4,128)S(1)} %get-tuple-element.20), channel_id=1, source_target_pairs={{0,16},{16,32},{32,48},{48,0},{1,17},{17,33},{33,49},{49,1},{2,18}... | collective-permute-start | bytes 147464 | tf_op jit(solution)/shard_map/ppermute | solution.py:225
  15.7 3.2 %collective-permute-start.4 = (f32[6,4,4,128]{3,2,1,0:T(4,128)S(1)}, f32[6,4,4,128]{3,2,1,0:T(4,128)S(1)}, u32[]{:S(2)}, u32[]{:S(2)}) collective-permute-start(f32[6,4,4,128]{3,2,1,0:T(4,128)S(1)} %get-tuple-element.26), channel_id=1, source_target_pairs={{0,1},{1,2},{2,3},{3,4},{4,5},{5,6},{6,7},{7,8},{8,9},{9,10},{10,1... | collective-permute-start | bytes 147464 | tf_op jit(solution)/shard_map/ppermute | solution.py:225
  18.9 2.5 %collective-permute-start.5 = (f32[6,4,4,128]{3,2,1,0:T(4,128)S(1)}, f32[6,4,4,128]{3,2,1,0:T(4,128)S(1)}, u32[]{:S(2)}, u32[]{:S(2)}) collective-permute-start(f32[6,4,4,128]{3,2,1,0:T(4,128)S(1)} %get-tuple-element.27), channel_id=1, source_target_pairs={{0,15},{1,0},{2,1},{3,2},{4,3},{5,4},{6,5},{7,6},{8,7},{9,8},{10,9... | collective-permute-start | bytes 147464 | tf_op jit(solution)/shard_map/ppermute | solution.py:225
  21.4 0.0 collective-permute-done.low_ref
  21.4 0.4 %rows.1.before_ref = f32[2,6,16,256]{3,2,1,0:T(8,128)S(1)} custom-call(f32[2,6,16,256]{3,2,1,0:T(8,128)S(1)} %get-tuple-element.18.prim_ref, f32[2,6,16,256]{3,2,1,0:T(8,128)S(1)} %collective-permute-done.low_ref, f32[2,6,16,256]{3,2,1,0:T(8,128)S(1)} %collective-permute-done.1.high_ref), custom_call_target="tpu_custom_call" | custom-call | tf_op jit(solution)/shard_map/rows/pallas_call | solution.py:239
  21.9 0.0 collective-permute-done.2.y_low
  21.9 0.0 copy-start.1
  21.9 0.9 %columns.1.change_ref = f32[2,6,16,256]{3,2,1,0:T(8,128)S(1)} custom-call(f32[2,6,16,256]{3,2,1,0:T(8,128)S(1)} %rows.1.before_ref, f32[6,4,16,128]{3,2,1,0:T(8,128)S(1)} %get-tuple-element.19.lines_y, f32[6,4,4,128]{3,2,1,0:T(4,128)S(1)} %collective-permute-done.2.y_low, f32[6,4,4,128]{3,2,1,0:T(4,128)S(1)} %collective-permute-done.3.y_high), custom_call_target="tpu_custom_call" | custom-call | tf_op jit(solution)/shard_map/columns/pallas_call | solution.py:242
  22.8 0.0 collective-permute-done.4.z_low
  22.8 0.0 copy-done.1
  22.8 0.7 %finish.1.own_ref = f32[2,6,16,256]{3,2,1,0:T(8,128)S(1)} custom-call(f32[2,6,16,256]{3,2,1,0:T(8,128)S(1)} %copy-done.1, f32[2,6,16,256]{3,2,1,0:T(8,128)S(1)} %columns.1.change_ref, f32[6,4,16,128]{3,2,1,0:T(8,128)S(1)} %get-tuple-element.25.lines_z, f32[6,4,4,128]{3,2,1,0:T(4,128)S(1)} %collective-permute-done.4.z_low, ...), custom_call_target="tpu_custom_call" | custom-call | tf_op jit(solution)/shard_map/finish/pallas_call | solution.py:251
  23.5 5.8 %collective-permute-start.6 = (f32[2,6,16,256]{3,2,1,0:T(8,128)S(1)}, f32[2,6,16,256]{3,2,1,0:T(8,128)S(1)}, u32[]{:S(2)}, u32[]{:S(2)}) collective-permute-start(f32[2,6,16,256]{3,2,1,0:T(8,128)S(1)} %finish.1.own_ref), channel_id=1, source_target_pairs={{0,1},{1,0},{2,3},{3,2},{4,5},{5,4},{6,7},{7,6},{8,9},{9,8},{10,11... | collective-permute-start | bytes 589832 | tf_op jit(solution)/shard_map/ppermute | solution.py:262
  29.3 0.0 copy-start.2
  29.3 0.6 %copy-done.2 = s32[32]{0:T(128)S(1)} copy-done((s32[32]{0:T(128)S(1)}, s32[32]{0:T(128)}, u32[]{:S(2)}) %copy-start.2) | copy-done | bytes 152
  30.0 0.1 select_reduce_fusion
  30.1 0.2 collective-permute-done.6.partner_ref
  30.3 0.1 broadcast_in_dim.8.code_ref
  30.4 0.8 %place.1 = f32[4,6,16,256]{3,2,1,0:T(8,128)} custom-call(s32[4,8,128]{2,1,0:T(8,128)S(1)} %broadcast_in_dim.8.code_ref, f32[2,6,16,256]{3,2,1,0:T(8,128)S(1)} %finish.1.own_ref, f32[2,6,16,256]{3,2,1,0:T(8,128)S(1)} %collective-permute-done.6.partner_ref), custom_call_target="tpu_custom_call" | custom-call | tf_op jit(solution)/shard_map/place/pallas_call | solution.py:263
  (9 shorter events, 0.0 us)
Async XLA Ops:
  0.0 21.4 %collective-permute-start = (f32[2,6,16,256]{3,2,1,0:T(8,128)}, f32[2,6,16,256]{3,2,1,0:T(8,128)S(1)}, u32[]{:S(2)}, u32[]{:S(2)}) collective-permute-start(f32[2,6,16,256]{3,2,1,0:T(8,128)} %u_ref.3), channel_id=1, source_target_pairs={{0,64},{64,128},{128,192},{192,256},{256,320},{320,384},{384,448},... | collective-permute-start | bytes 589832 | tf_op jit(solution)/shard_map/ppermute | solution.py:225
  4.0 17.4 %collective-permute-start.1 = (f32[2,6,16,256]{3,2,1,0:T(8,128)}, f32[2,6,16,256]{3,2,1,0:T(8,128)S(1)}, u32[]{:S(2)}, u32[]{:S(2)}) collective-permute-start(f32[2,6,16,256]{3,2,1,0:T(8,128)} %u_ref.3), channel_id=1, source_target_pairs={{0,448},{64,0},{128,64},{192,128},{256,192},{320,256},{384,320},{4... | collective-permute-start | bytes 589832 | tf_op jit(solution)/shard_map/ppermute | solution.py:225
  7.9 0.9 %copy-start = (f32[2,6,16,256]{3,2,1,0:T(8,128)S(1)}, f32[2,6,16,256]{3,2,1,0:T(8,128)}, u32[]{:S(2)}) copy-start(f32[2,6,16,256]{3,2,1,0:T(8,128)} %u_ref.3) | copy-start | bytes 589828
  9.4 6.3 %collective-permute-start.3 = (f32[6,4,4,128]{3,2,1,0:T(4,128)S(1)}, f32[6,4,4,128]{3,2,1,0:T(4,128)S(1)}, u32[]{:S(2)}, u32[]{:S(2)}) collective-permute-start(f32[6,4,4,128]{3,2,1,0:T(4,128)S(1)} %get-tuple-element.23), channel_id=1, source_target_pairs={{0,48},{16,0},{32,16},{48,32},{1,49},{17,1},{33,17},{49,33},{2,50}... | collective-permute-start | bytes 147464 | tf_op jit(solution)/shard_map/ppermute | solution.py:225
  13.7 8.1 %collective-permute-start.2 = (f32[6,4,4,128]{3,2,1,0:T(4,128)S(1)}, f32[6,4,4,128]{3,2,1,0:T(4,128)S(1)}, u32[]{:S(2)}, u32[]{:S(2)}) collective-permute-start(f32[6,4,4,128]{3,2,1,0:T(4,128)S(1)} %get-tuple-element.20), channel_id=1, source_target_pairs={{0,16},{16,32},{32,48},{48,0},{1,17},{17,33},{33,49},{49,1},{2,18}... | collective-permute-start | bytes 147464 | tf_op jit(solution)/shard_map/ppermute | solution.py:225
  15.7 7.0 %collective-permute-start.4 = (f32[6,4,4,128]{3,2,1,0:T(4,128)S(1)}, f32[6,4,4,128]{3,2,1,0:T(4,128)S(1)}, u32[]{:S(2)}, u32[]{:S(2)}) collective-permute-start(f32[6,4,4,128]{3,2,1,0:T(4,128)S(1)} %get-tuple-element.26), channel_id=1, source_target_pairs={{0,1},{1,2},{2,3},{3,4},{4,5},{5,6},{6,7},{7,8},{8,9},{9,10},{10,1... | collective-permute-start | bytes 147464 | tf_op jit(solution)/shard_map/ppermute | solution.py:225
  18.9 3.8 %collective-permute-start.5 = (f32[6,4,4,128]{3,2,1,0:T(4,128)S(1)}, f32[6,4,4,128]{3,2,1,0:T(4,128)S(1)}, u32[]{:S(2)}, u32[]{:S(2)}) collective-permute-start(f32[6,4,4,128]{3,2,1,0:T(4,128)S(1)} %get-tuple-element.27), channel_id=1, source_target_pairs={{0,15},{1,0},{2,1},{3,2},{4,3},{5,4},{6,5},{7,6},{8,7},{9,8},{10,9... | collective-permute-start | bytes 147464 | tf_op jit(solution)/shard_map/ppermute | solution.py:225
  21.9 0.9 %copy-start.1 = (f32[2,6,16,256]{3,2,1,0:T(8,128)S(1)}, f32[2,6,16,256]{3,2,1,0:T(8,128)}, u32[]{:S(2)}) copy-start(f32[2,6,16,256]{3,2,1,0:T(8,128)} %u_ref.3) | copy-start | bytes 589828
  22.8 6.5 %copy-start.3 = (s32[32]{0:T(128)S(1)}, s32[32]{0:T(128)}, u32[]{:S(2)}) copy-start(s32[32]{0:T(128)} %param.4) | copy-start | bytes 388
  23.5 6.8 %collective-permute-start.6 = (f32[2,6,16,256]{3,2,1,0:T(8,128)S(1)}, f32[2,6,16,256]{3,2,1,0:T(8,128)S(1)}, u32[]{:S(2)}, u32[]{:S(2)}) collective-permute-start(f32[2,6,16,256]{3,2,1,0:T(8,128)S(1)} %finish.1.own_ref), channel_id=1, source_target_pairs={{0,1},{1,0},{2,3},{3,2},{4,5},{5,4},{6,7},{7,6},{8,9},{9,8},{10,11... | collective-permute-start | bytes 589832 | tf_op jit(solution)/shard_map/ppermute | solution.py:262
  29.3 0.7 %copy-start.2 = (s32[32]{0:T(128)S(1)}, s32[32]{0:T(128)}, u32[]{:S(2)}) copy-start(s32[32]{0:T(128)} %param.5) | copy-start | bytes 388
